TPU v7x, 32 devices: a whole 2x2x4 slice. The times are simulated.
32 devices in a mesh: grp: 4 (over z), node: 8 (over y, x, core).
Axes of the slice: x: 2, y: 2, z: 4, core: 2. Of those that a mesh axis runs over, the one named last changes fastest.
Arguments:
- features: bfloat16 [8, 4096, 100], P('grp', 'node')
- adjacency: bfloat16 [8, 4096, 4096], P('grp', 'node'), as said below
- labels: int32 [8, 4096], P('grp', 'node'), may hold values from 0 to 46
- train_mask: int32 [8, 4096], P('grp', 'node'), may hold values from 0 to 1, as said below
- input_weight: float32 [100, 256], P(None, 'grp'), may hold values from -0.625 to 0.625
- input_moment: float32 [100, 256], P(None, 'grp'), may hold values from -0.125 to 0.125
- conv_weight: float32 [2, 512, 256], P(None, None, 'grp'), may hold values from -0.25 to 0.25
- conv_moment: float32 [2, 512, 256], P(None, None, 'grp'), may hold values from -0.125 to 0.125
- head_weight: float32 [256, 47], replicated, may hold values from -0.375 to 0.375
- head_first: float32 [256, 47], replicated, may hold values from -0.013671875 to 0.013671875
- head_second: float32 [256, 47], replicated, may hold values from 3.2348632e-06 to 1.2817382e-05
- head_bias: float32 [47], replicated, may hold values from -3 to 3
- bias_first: float32 [47], replicated, may hold values from -0.013671875 to 0.013671875
- bias_second: float32 [47], replicated, may hold values from 3.2348632e-06 to 1.2817382e-05
- norm_params: float32 [2, 2, 256], replicated
- norm_first: float32 [2, 2, 256], replicated, may hold values from -0.013671875 to 0.013671875
- norm_second: float32 [2, 2, 256], replicated, may hold values from 3.2348632e-06 to 1.2817382e-05
Outputs:
- loss_parts: float32 [2], replicated
- input_new: float32 [100, 256], P(None, 'grp')
- input_moment_new: float32 [100, 256], P(None, 'grp')
- conv_new: float32 [2, 512, 256], P(None, None, 'grp')
- conv_moment_new: float32 [2, 512, 256], P(None, None, 'grp')
- head_new: float32 [256, 47], replicated
- head_first_new: float32 [256, 47], replicated
- head_second_new: float32 [256, 47], replicated
- bias_new: float32 [47], replicated
- bias_first_new: float32 [47], replicated
- bias_second_new: float32 [47], replicated
- norm_new: float32 [2, 2, 256], replicated
- norm_first_new: float32 [2, 2, 256], replicated
- norm_second_new: float32 [2, 2, 256], replicated
Inputs may be any that keep to these rules, and one draw needn't show every extreme that they name: adjacency[s] equals its own transpose for every subgraph s; entries are zero or positive. `train_mask`: 0 or 1; the first node of every subgraph is a training node.
All inputs are finite; a program needn't handle non-finite values.
Results may differ from a plain program's by a relative error of at most 0.003.
Values may be sent and summed in bfloat16 or wider, within the bound.
A program may use at most 192 MiB of HBM per device.

v0:
```python
import jax
import jax.numpy as jnp
from jax import lax
from jax.sharding import PartitionSpec as P

NS_STEPS = 5
STEP = 10


norm_eps = 1e-05
smoothing = 0.1
poly_first = 3.4445
poly_second = -4.775
poly_third = 2.0315
muon_beta = 0.95
muon_rate = 0.2
decay_rate = 0.01
adam_rate = 0.05
beta_first = 0.9
beta_second = 0.95
adam_eps = 1e-08


def lowered(value):
    return value.astype(jnp.bfloat16)


def matmul_hi(left, right):
    return jnp.dot(left, right, precision=lax.Precision.HIGHEST)


def column_dot(left, right):
    return lax.dot_general(
        left, right, (((0,), (0,)), ((), ())), preferred_element_type=jnp.float32
    )


def row_dot(left, right):
    return lax.dot_general(
        left, right, (((1,), (1,)), ((), ())), preferred_element_type=jnp.float32
    )


def neighbour_sum(adj, values):
    return jnp.dot(
        adj, lax.all_gather(values, "node", axis=0, tiled=True), preferred_element_type=jnp.float32
    )


def neighbour_back(adj, grads):
    return lax.psum_scatter(column_dot(adj, grads), "node", scatter_dimension=0, tiled=True)


def layer_forward(adj, inputs_low, weight_low, gain, shift, total_rows):
    hidden = weight_low.shape[1]
    agg_low = lowered(neighbour_sum(adj, inputs_low))
    pre = jnp.dot(inputs_low, weight_low[:hidden], preferred_element_type=jnp.float32)
    pre = pre + jnp.dot(agg_low, weight_low[hidden:], preferred_element_type=jnp.float32)
    act = jax.nn.gelu(pre)
    sums, squares = lax.psum((jnp.sum(act, 0), jnp.sum(act * act, 0)), "node")
    mean = sums / total_rows
    var = squares / total_rows - mean * mean
    inv_std = lax.rsqrt(var + norm_eps)
    normed = (act - mean) * inv_std
    return (normed * gain + shift, (inputs_low, agg_low, pre, normed, inv_std))


def layer_backward(adj, weight_low, gain, kept, grad_out, total_rows):
    inputs_low, agg_low, pre, normed, inv_std = kept
    hidden = weight_low.shape[1]
    grad_gain = jnp.sum(grad_out * normed, 0)
    grad_shift = jnp.sum(grad_out, 0)
    grad_normed = grad_out * gain
    first, second = lax.psum((jnp.sum(grad_normed, 0), jnp.sum(grad_normed * normed, 0)), "node")
    grad_act = (grad_normed - first / total_rows - normed * (second / total_rows)) * inv_std
    grad_pre = jax.vjp(jax.nn.gelu, pre)[1](grad_act)[0]
    pre_low = lowered(grad_pre)
    grad_weight = jnp.concatenate(
        [column_dot(inputs_low, pre_low), column_dot(agg_low, pre_low)], 0
    )
    grad_agg = lowered(row_dot(pre_low, weight_low[hidden:]))
    grad_inputs = row_dot(pre_low, weight_low[:hidden]) + neighbour_back(adj, grad_agg)
    return (grad_inputs, grad_weight, jnp.stack([grad_gain, grad_shift]))


def gram_of(block):
    return matmul_hi(block, block.T)


def orthogonal_blocks(first_block, second_block, third_block):
    blocks = [first_block, second_block, third_block]
    for step in range(NS_STEPS):
        grams = lax.psum((gram_of(blocks[0]), gram_of(blocks[1]), gram_of(blocks[2])), "grp")
        grams = list(grams)
        if step == 0:
            scales = [jnp.sqrt(jnp.trace(gram)) + 1e-07 for gram in grams]
            blocks = [block / scale for block, scale in zip(blocks, scales)]
            grams = [gram / (scale * scale) for gram, scale in zip(grams, scales)]
        polys = [poly_second * gram + poly_third * matmul_hi(gram, gram) for gram in grams]
        blocks = [poly_first * block + matmul_hi(poly, block) for block, poly in zip(blocks, polys)]
    return blocks


def adamw(weight, grad, first, second):
    first_new = beta_first * first + (1.0 - beta_first) * grad
    second_new = beta_second * second + (1.0 - beta_second) * grad * grad
    fixed_first = first_new / (1.0 - beta_first**STEP)
    fixed_second = second_new / (1.0 - beta_second**STEP)
    update = fixed_first / (jnp.sqrt(fixed_second) + adam_eps) + decay_rate * weight
    return (weight - adam_rate * update, first_new, second_new)


def per_device(
    features,
    adjacency,
    labels,
    train_mask,
    input_weight,
    input_moment,
    conv_weight,
    conv_moment,
    head_weight,
    head_first,
    head_second,
    head_bias,
    bias_first,
    bias_second,
    norm_params,
    norm_first,
    norm_second,
):
    layers = conv_weight.shape[0]
    hidden = head_weight.shape[0]
    classes = head_weight.shape[1]
    f_width = input_weight.shape[0]
    total_rows = features.shape[1] * lax.axis_size("node")
    input_full, conv_full = (
        lax.all_gather(lowered(input_weight), "grp", axis=1, tiled=True),
        lax.all_gather(lowered(conv_weight), "grp", axis=2, tiled=True),
    )
    head_low = lowered(head_weight)
    count = lax.psum(jnp.sum(train_mask).astype(jnp.float32), ("grp", "node"))
    grad_input = jnp.zeros((f_width, hidden), jnp.float32)
    grad_conv = [jnp.zeros((2 * hidden, hidden), jnp.float32) for layer in range(layers)]
    grad_norm = [jnp.zeros((2, hidden), jnp.float32) for layer in range(layers)]
    grad_head = jnp.zeros((hidden, classes), jnp.float32)
    grad_bias = jnp.zeros((classes,), jnp.float32)
    loss_sum = jnp.float32(0.0)
    for graph in range(features.shape[0]):
        inputs = features[graph]
        adj = adjacency[graph]
        current_low = lowered(jnp.dot(inputs, input_full, preferred_element_type=jnp.float32))
        kept_list = []
        for layer in range(layers):
            output, kept = layer_forward(
                adj,
                current_low,
                conv_full[layer],
                norm_params[layer, 0],
                norm_params[layer, 1],
                total_rows,
            )
            kept_list.append(kept)
            current_low = lowered(output)
        logits = jnp.dot(current_low, head_low, preferred_element_type=jnp.float32) + head_bias
        logp = jax.nn.log_softmax(logits, -1)
        onehot = (labels[graph][:, None] == jnp.arange(classes, dtype=jnp.int32)[None, :]).astype(
            jnp.float32
        )
        target = (1.0 - smoothing) * onehot + smoothing / classes
        weights = train_mask[graph].astype(jnp.float32)
        loss_sum = loss_sum - jnp.sum(weights * jnp.sum(target * logp, -1))
        logits_low = lowered((weights / count)[:, None] * (jnp.exp(logp) - target))
        grad_head = grad_head + column_dot(current_low, logits_low)
        grad_bias = grad_bias + jnp.sum(logits_low.astype(jnp.float32), 0)
        grad_low = lowered(row_dot(logits_low, head_low))
        for layer in reversed(range(layers)):
            grad_inputs, grad_weight, grad_pair = layer_backward(
                adj,
                conv_full[layer],
                norm_params[layer, 0],
                kept_list[layer],
                grad_low.astype(jnp.float32),
                total_rows,
            )
            grad_conv[layer] = grad_conv[layer] + grad_weight
            grad_norm[layer] = grad_norm[layer] + grad_pair
            grad_low = lowered(grad_inputs)
        grad_input = grad_input + column_dot(inputs, grad_low)
    grad_conv_all = jnp.stack(grad_conv)
    grad_norm_all = jnp.stack(grad_norm)
    grad_input, grad_conv_all, grad_head, grad_bias, grad_norm_all, loss_sum = lax.psum(
        (grad_input, grad_conv_all, grad_head, grad_bias, grad_norm_all, loss_sum), "node"
    )
    grad_input, grad_conv_all = (
        lax.psum_scatter(grad_input, "grp", scatter_dimension=1, tiled=True),
        lax.psum_scatter(grad_conv_all, "grp", scatter_dimension=2, tiled=True),
    )
    grad_head, grad_bias, grad_norm_all, loss_sum = lax.psum(
        (grad_head, grad_bias, grad_norm_all, loss_sum), "grp"
    )
    moment_in = muon_beta * input_moment + grad_input
    moment_conv = muon_beta * conv_moment + grad_conv_all
    ortho_in, ortho_first, ortho_second = orthogonal_blocks(
        moment_in, moment_conv[0], moment_conv[1]
    )
    factor_in = 0.2 * float(max(f_width, hidden)) ** 0.5
    factor_conv = 0.2 * float(2 * hidden) ** 0.5
    input_new = input_weight - muon_rate * (factor_in * ortho_in + decay_rate * input_weight)
    ortho_conv = jnp.stack([ortho_first, ortho_second])
    conv_new = conv_weight - muon_rate * (factor_conv * ortho_conv + decay_rate * conv_weight)
    head_new, head_first_new, head_second_new = adamw(
        head_weight, grad_head, head_first, head_second
    )
    bias_new, bias_first_new, bias_second_new = adamw(head_bias, grad_bias, bias_first, bias_second)
    norm_new, norm_first_new, norm_second_new = adamw(
        norm_params, grad_norm_all, norm_first, norm_second
    )
    loss_parts = jnp.stack([loss_sum, count])
    return (
        loss_parts,
        input_new,
        moment_in,
        conv_new,
        moment_conv,
        head_new,
        head_first_new,
        head_second_new,
        bias_new,
        bias_first_new,
        bias_second_new,
        norm_new,
        norm_first_new,
        norm_second_new,
    )


def solution(mesh):
    placed = (
        P("grp", "node", None),
        P("grp", "node", None),
        P("grp", "node"),
        P("grp", "node"),
        P(None, "grp"),
        P(None, "grp"),
        P(None, None, "grp"),
        P(None, None, "grp"),
        P(),
        P(),
        P(),
        P(),
        P(),
        P(),
        P(),
        P(),
        P(),
    )
    return jax.shard_map(
        per_device,
        mesh=mesh,
        in_specs=placed,
        out_specs=(
            P(),
            P(None, "grp"),
            P(None, "grp"),
            P(None, None, "grp"),
            P(None, None, "grp"),
            P(),
            P(),
            P(),
            P(),
            P(),
            P(),
            P(),
            P(),
            P(),
        ),
        check_vma=False,
    )
```

profile of v0, /device:TPU:0, one launch (start us, length us, event | category | flops | bytes accessed | tf_op | source)
XLA Modules:
  0.0 1087.1 jit_solution(4181715431514675727)
XLA Ops:
  8.0 14.9 %all_gather.18 = bf16[100,256]{0,1:T(8,128)(2,1)S(1)} all-gather(bf16[100,64]{0,1:T(8,128)(2,1)S(1)} %convert_element_type.136), channel_id=1, replica_groups=mesh['grp'=4,'node'=8] {'grp'}, dimensions={1}, use_global_device_ids=true | all-gather | bytes 64000 | tf_op jit(solution)/shard_map/all_gather | solution.py:138
  27.3 16.0 %all_gather.19 = bf16[2,512,256]{1,2,0:T(8,128)(2,1)S(1)} all-gather(bf16[2,512,64]{1,2,0:T(8,128)(2,1)S(1)} %convert_element_type.138), channel_id=1, replica_groups=mesh['grp'=4,'node'=8] {'grp'}, dimensions={2}, use_global_device_ids=true | all-gather | bytes 655360 | tf_op jit(solution)/shard_map/all_gather | solution.py:139
  47.1 7.3 all-gather.5.cloned.1.call-done
  54.4 4.1 fusion.32
  59.0 25.8 %all-gather.9.cloned.1.call-done = bf16[4096,256]{1,0:T(8,128)(2,1)} async-done(((bf16[512,256]{1,0:T(8,128)(2,1)}), bf16[4096,256]{1,0:T(8,128)(2,1)}) %all-gather.9.cloned.1.call-update) | async-done | bytes 2097168 | tf_op jit(solution)/shard_map/all_gather | solution.py:46
  84.8 4.1 fusion.38
  89.4 13.1 %all-reduce.5 = (f32[256]{0:T(256)S(1)}, f32[256]{0:T(256)S(1)}, f32[256]{0:T(256)S(1)}, f32[256]{0:T(256)S(1)}) all-reduce(f32[256]{0:T(256)S(1)} %get-tuple-element.66, f32[256]{0:T(256)S(1)} %get-tuple-element.65, f32[256]{0:T(256)S(1)} %get-tuple-element.62, f32[256]{0:T(256)S(1)} %get-tuple-element.61), channel_id=1, replica_groups=mesh['grp'=4,'node'=8] {'node'}, use_global_device_ids=true, to_apply=%region_3.0 | all-reduce | flops 1024 | bytes 8192 | tf_op jit(solution)/shard_map/psum | solution.py:60
  105.9 39.4 %psum.304 = f32[]{:T(128)} all-reduce(f32[]{:T(128)S(6)} %convert_element_type.151), channel_id=1, replica_groups=mesh['grp'=4,'node'=8] {'grp','node'}, use_global_device_ids=true, to_apply=%region_25.0 | all-reduce | flops 1 | bytes 8 | tf_op jit(solution)/shard_map/psum | solution.py:142
  150.3 4.4 fusion.41
  156.4 5.6 all-gather.7.cloned.1.call-done
  162.0 4.1 fusion.35
  167.2 13.3 %all-reduce.4 = (f32[256]{0:T(256)S(1)}, f32[256]{0:T(256)S(1)}, f32[256]{0:T(256)S(1)}, f32[256]{0:T(256)S(1)}) all-reduce(f32[256]{0:T(256)} %get-tuple-element.64, f32[256]{0:T(256)} %get-tuple-element.63, f32[256]{0:T(256)} %get-tuple-element.60, f32[256]{0:T(256)} %get-tuple-element.59), channel_id=1, replica_groups=mesh['grp'=4,'node'=8] {'node'}, use_global_device_ids=true, to_apply=%region_7.0 | all-reduce | flops 1024 | bytes 8192 | tf_op jit(solution)/shard_map/psum | solution.py:60
  186.7 2.8 multiply_reduce_fusion.1
  189.5 12.6 %all-reduce.3 = (f32[256]{0:T(256)}, f32[256]{0:T(256)}, f32[256]{0:T(256)}, f32[256]{0:T(256)}) all-reduce(f32[256]{0:T(256)} %get-tuple-element.140, f32[256]{0:T(256)} %get-tuple-element.139, f32[256]{0:T(256)} %get-tuple-element.50, f32[256]{0:T(256)} %get-tuple-element.51), channel_id=1, replica_groups=mesh['grp'=4,'node'=8] {'node'}, use_global_device_ids=true, to_apply=%region_39.0 | all-reduce | flops 1024 | bytes 8192 | tf_op jit(solution)/shard_map/psum | solution.py:74
  204.8 2.2 fusion.80
  207.0 5.9 convolution_bitcast_fusion.1
  213.0 5.9 convolution_bitcast_fusion.3
  220.9 43.5 %reduce-scatter.12.cloned.1.call-done = f32[512,256]{1,0:T(8,128)} async-done(((f32[4096,256]{1,0:T(8,128)}), f32[512,256]{1,0:T(8,128)}) %reduce-scatter.12.cloned.1.call-update) | async-done | bytes 524304 | tf_op jit(solution)/shard_map/reduce_scatter | solution.py:51
  264.4 2.1 fusion.48
  266.6 52.8 %reduce-scatter.8.cloned.1.call-done = f32[512,256]{1,0:T(8,128)} async-done(((f32[4096,256]{1,0:T(8,128)}), f32[512,256]{1,0:T(8,128)}) %reduce-scatter.8.cloned.1.call-update) | async-done | bytes 524304 | tf_op jit(solution)/shard_map/reduce_scatter | solution.py:51
  319.4 3.2 multiply_reduce_fusion.3
  322.6 12.7 %all-reduce.2 = (f32[256]{0:T(256)S(1)}, f32[256]{0:T(256)S(1)}, f32[256]{0:T(256)S(1)}, f32[256]{0:T(256)S(1)}) all-reduce(f32[256]{0:T(256)S(1)} %get-tuple-element.134, f32[256]{0:T(256)S(1)} %get-tuple-element.133, f32[256]{0:T(256)S(1)} %get-tuple-element.46, ...), channel_id=1, replica_groups=mesh['grp'=4,'node'=8] {'node'}, use_global_device_ids=true, to_apply=%region_44.0 | all-reduce | flops 1024 | bytes 8192 | tf_op jit(solution)/shard_map/psum | solution.py:74
  335.3 2.2 fusion.73
  343.3 50.6 %all-reduce.24.cloned.1.call-done = f32[2,512,256]{1,0,2:T(2,128)} async-done(((f32[2,512,256]{1,0,2:T(2,128)}), f32[2,512,256]{1,0,2:T(2,128)}) %all-reduce.24.cloned.1.call-update) | async-done | bytes 1048592
  395.7 55.1 %all-reduce.22.cloned.1.call-done = f32[2,512,64]{1,2,0:T(8,128)} async-done(((f32[2,512,64]{1,2,0:T(8,128)}), f32[2,512,64]{1,2,0:T(8,128)}) %all-reduce.22.cloned.1.call-update) | async-done | bytes 262160 | tf_op jit(solution)/shard_map/psum | solution.py:192
  451.8 2.0 fusion.103
  453.8 2.0 fusion.102
  456.3 86.1 %all-reduce.34.cloned.1.call-done = (f32[512,512]{1,0:T(8,128)}, f32[512,512]{1,0:T(8,128)}) async-done(((f32[512,512]{1,0:T(8,128)}, f32[512,512]{1,0:T(8,128)}), (f32[512,512]{1,0:T(8,128)}, f32[512,512]{1,0:T(8,128)})) %all-reduce.34.cloned.1.call-update) | async-done | bytes 2097168 | tf_op jit(solution)/shard_map/psum | solution.py:93
  542.5 1.9 select_reduce_fusion.1
  545.1 1.9 select_reduce_fusion
  547.7 4.0 fusion.24
  552.8 2.0 fusion.29
  555.9 2.0 fusion.135
  557.9 2.0 fusion.139
  560.0 5.9 convolution_bitcast_fusion
  566.0 5.9 convolution_bitcast_fusion.2
  572.2 74.0 %all-reduce.32.cloned.1.call-done = (f32[512,512]{1,0:T(8,128)}, f32[512,512]{1,0:T(8,128)}) async-done(((f32[512,512]{1,0:T(8,128)}, f32[512,512]{1,0:T(8,128)}), (f32[512,512]{1,0:T(8,128)}, f32[512,512]{1,0:T(8,128)})) %all-reduce.32.cloned.1.call-update) | async-done | bytes 2097168 | tf_op jit(solution)/shard_map/psum | solution.py:93
  646.2 4.2 fusion.23
  651.5 2.1 fusion.140
  653.6 1.9 fusion.28
  656.9 43.0 %reduce-scatter.14.cloned.1.call-done = f32[512,256]{1,0:T(8,128)} async-done(((f32[4096,256]{1,0:T(8,128)}), f32[512,256]{1,0:T(8,128)}) %reduce-scatter.14.cloned.1.call-update) | async-done | bytes 524304 | tf_op jit(solution)/shard_map/reduce_scatter | solution.py:51
  701.3 53.5 %reduce-scatter.10.cloned.1.call-done = f32[512,256]{1,0:T(8,128)} async-done(((f32[4096,256]{1,0:T(8,128)}), f32[512,256]{1,0:T(8,128)}) %reduce-scatter.10.cloned.1.call-update) | async-done | bytes 524304 | tf_op jit(solution)/shard_map/reduce_scatter | solution.py:51
  757.1 2.0 fusion.136
  762.8 14.0 %reduce-scatter.16.cloned.1.call-done = f32[64,100]{1,0:T(8,128)} async-done(((f32[256,100]{1,0:T(8,128)}), f32[64,100]{1,0:T(8,128)}) %reduce-scatter.16.cloned.1.call-update) | async-done | bytes 25616
  776.8 25.1 %all-reduce.35 = (f32[]{:T(128)}, f32[100,64]{0,1:T(8,128)S(1)}, f32[256,47]{0,1:T(8,128)S(1)}, f32[47]{0:T(128)S(1)}, f32[2,2,256]{2,1,0:T(2,128)S(1)}) all-reduce(f32[]{:T(128)S(6)} %sub.156, f32[100,64]{0,1:T(8,128)} %bitcast.267, f32[256,47]{0,1:T(8,128)S(1)} %convolution_add_fusion.20, ...), channel_id=1, replica_groups=mesh['grp'=4,'node'=8] {'node'}, use_global_device_ids=true, to_apply=%region_22.0 | all-reduce | flops 19504 | bytes 156032 | tf_op jit(solution)/shard_map/psum | solution.py:192
  802.0 62.4 %all-reduce.30.cloned.1.call-done = (f32[512,512]{1,0:T(8,128)}, f32[512,512]{1,0:T(8,128)}) async-done(((f32[512,512]{1,0:T(8,128)}, f32[512,512]{1,0:T(8,128)}), (f32[512,512]{1,0:T(8,128)}, f32[512,512]{1,0:T(8,128)})) %all-reduce.30.cloned.1.call-update) | async-done | bytes 2097168 | tf_op jit(solution)/shard_map/psum | solution.py:93
  864.4 4.1 fusion.22
  869.6 2.1 fusion.141
  871.7 1.9 fusion.27
  874.7 2.0 fusion.137
  877.1 19.6 %psum.314 = f32[100,100]{1,0:T(8,128)S(1)} all-reduce(f32[100,100]{1,0:T(8,128)S(1)} %fusion.130), channel_id=1, replica_groups=mesh['grp'=4,'node'=8] {'grp'}, use_global_device_ids=true, to_apply=%region_48.0 | all-reduce | flops 10000 | bytes 80000 | tf_op jit(solution)/shard_map/psum | solution.py:93
  898.8 20.3 %psum.315 = f32[100,100]{1,0:T(8,128)S(1)} all-reduce(f32[100,100]{1,0:T(8,128)S(1)} %fusion.131), channel_id=1, replica_groups=mesh['grp'=4,'node'=8] {'grp'}, use_global_device_ids=true, to_apply=%region_50.0 | all-reduce | flops 10000 | bytes 80000 | tf_op jit(solution)/shard_map/psum | solution.py:93
  919.9 19.1 %psum.316 = f32[100,100]{1,0:T(8,128)S(1)} all-reduce(f32[100,100]{1,0:T(8,128)S(1)} %fusion.132), channel_id=1, replica_groups=mesh['grp'=4,'node'=8] {'grp'}, use_global_device_ids=true, to_apply=%region_51.0 | all-reduce | flops 10000 | bytes 80000 | tf_op jit(solution)/shard_map/psum | solution.py:93
  939.5 27.9 %all-reduce.28.cloned.1.call-done = (f32[512,512]{1,0:T(8,128)}, f32[512,512]{1,0:T(8,128)}) async-done(((f32[512,512]{1,0:T(8,128)}, f32[512,512]{1,0:T(8,128)}), (f32[512,512]{1,0:T(8,128)}, f32[512,512]{1,0:T(8,128)})) %all-reduce.28.cloned.1.call-update) | async-done | bytes 2097168 | tf_op jit(solution)/shard_map/psum | solution.py:93
  967.4 3.9 fusion.21
  972.4 2.1 fusion.142
  974.6 1.9 fusion.26
  977.6 2.0 fusion.138
  980.0 19.2 %psum.317 = f32[100,100]{1,0:T(8,128)S(1)} all-reduce(f32[100,100]{1,0:T(8,128)S(1)} %fusion.133), channel_id=1, replica_groups=mesh['grp'=4,'node'=8] {'grp'}, use_global_device_ids=true, to_apply=%region_52.0 | all-reduce | flops 10000 | bytes 80000 | tf_op jit(solution)/shard_map/psum | solution.py:93
  999.9 23.7 %all-reduce.36 = (f32[1]{0:T(128)}, f32[100,100]{1,0:T(8,128)S(1)}, f32[256,47]{0,1:T(8,128)S(1)}, f32[47]{0:T(128)S(1)}, f32[2,2,256]{2,1,0:T(2,128)S(1)}) all-reduce(f32[1]{0:T(128)} %bitcast.16, f32[100,100]{1,0:T(8,128)S(1)} %fusion.134, f32[256,47]{0,1:T(8,128)S(1)} %get-tuple-element.69, ...), channel_id=1, replica_groups=mesh['grp'=4,'node'=8] {'grp'}, use_global_device_ids=true, to_apply=%region_23.0 | all-reduce | flops 23104 | bytes 184832 | tf_op jit(solution)/shard_map/psum | solution.py:199
  1023.7 1.9 pad_maximum_fusion.2
  1028.5 42.7 %all-reduce.26.cloned.1.call-done = (f32[512,512]{1,0:T(8,128)}, f32[512,512]{1,0:T(8,128)}) async-done(((f32[512,512]{1,0:T(8,128)}, f32[512,512]{1,0:T(8,128)}), (f32[512,512]{1,0:T(8,128)}, f32[512,512]{1,0:T(8,128)})) %all-reduce.26.cloned.1.call-update) | async-done | bytes 2097168 | tf_op jit(solution)/shard_map/psum | solution.py:93
  1071.2 3.9 fusion.20
  1076.2 1.9 fusion.25
  (281 shorter events, 64.7 us)
Async XLA Ops:
  7.2 47.2 %all-gather.5.cloned.1.call-start = ((), (), s32[]{:S(2)}) async-start(), calls=%async_computation.5 | async-start | bytes 2359296 | tf_op jit(solution)/shard_map/all_gather | solution.py:46
  25.2 59.6 %all-gather.9.cloned.1.call-start = ((), (), s32[]{:S(2)}) async-start(), calls=%async_computation.7 | async-start | bytes 2359296 | tf_op jit(solution)/shard_map/all_gather | solution.py:46
  26.3 123.9 %all-gather.11.cloned.1.call-start = ((), (), s32[]{:S(2)}) async-start(), calls=%async_computation.8 | async-start | bytes 2359296 | tf_op jit(solution)/shard_map/all_gather | solution.py:46
  44.7 57.9 %copy-start.39 = (f32[1,1,256]{2,1,0:T(1,128)}, f32[1,1,256]{2,1,0:T(1,128)S(1)}, u32[]{:S(2)}) copy-start(f32[1,1,256]{2,1,0:T(1,128)S(1)} %get-tuple-element.124) | copy-start | bytes 3076
  58.5 30.4 %copy-start.17 = (bf16[256,512]{1,0:T(8,128)(2,1)}, bf16[256,512]{1,0:T(8,128)(2,1)S(1)}, u32[]{:S(2)}) copy-start(bf16[256,512]{1,0:T(8,128)(2,1)S(1)} %fusion.32) | copy-start | bytes 786436
  88.9 58.8 %copy-start.18 = (bf16[256,512]{1,0:T(8,128)(2,1)}, bf16[256,512]{1,0:T(8,128)(2,1)S(1)}, u32[]{:S(2)}) copy-start(bf16[256,512]{1,0:T(8,128)(2,1)S(1)} %fusion.38) | copy-start | bytes 786436
  89.0 56.3 %copy-start.25 = (f32[256,47]{0,1:T(8,128)S(1)}, f32[256,47]{0,1:T(8,128)}, u32[]{:S(2)}) copy-start(f32[256,47]{0,1:T(8,128)} %param.26) | copy-start | bytes 144388
  89.0 56.9 %copy-start.59 = (s32[2,512]{1,0:T(2,128)S(1)}, s32[2,512]{1,0:T(2,128)}, u32[]{:S(2)}) copy-start(s32[2,512]{1,0:T(2,128)} %param.20) | copy-start | bytes 12292
  102.6 47.7 %copy-start.40 = (f32[256]{0:T(256)}, f32[256]{0:T(256)S(1)}, u32[]{:S(2)}) copy-start(f32[256]{0:T(256)S(1)} %get-tuple-element.146) | copy-start | bytes 3076
  102.6 47.7 %copy-start.41 = (f32[256]{0:T(256)}, f32[256]{0:T(256)S(1)}, u32[]{:S(2)}) copy-start(f32[256]{0:T(256)S(1)} %get-tuple-element.147) | copy-start | bytes 3076
  102.6 47.7 %copy-start.42 = (f32[256]{0:T(256)}, f32[256]{0:T(256)S(1)}, u32[]{:S(2)}) copy-start(f32[256]{0:T(256)S(1)} %get-tuple-element.162) | copy-start | bytes 3076
  102.6 47.7 %copy-start.43 = (f32[256]{0:T(256)}, f32[256]{0:T(256)S(1)}, u32[]{:S(2)}) copy-start(f32[256]{0:T(256)S(1)} %get-tuple-element.163) | copy-start | bytes 3076
  104.0 58.0 %all-gather.7.cloned.1.call-start = ((), (), s32[]{:S(2)}) async-start(), calls=%async_computation.6 | async-start | bytes 2359296 | tf_op jit(solution)/shard_map/all_gather | solution.py:46
  104.5 159.9 %reduce-scatter.12.cloned.1.call-start = ((), (), s32[]{:S(2)}) async-start(), calls=%async_computation.11 | async-start | bytes 4718592 | tf_op jit(solution)/shard_map/reduce_scatter | solution.py:51
  156.4 48.4 %copy-start.11 = (f32[512,256]{1,0:T(8,128)}, f32[512,256]{1,0:T(8,128)S(1)}, u32[]{:S(2)}) copy-start(f32[512,256]{1,0:T(8,128)S(1)} %get-tuple-element.153) | copy-start | bytes 1572868
  167.2 37.6 %copy-start.13 = (f32[512,256]{1,0:T(8,128)}, f32[512,256]{1,0:T(8,128)S(1)}, u32[]{:S(2)}) copy-start(f32[512,256]{1,0:T(8,128)S(1)} %get-tuple-element.152) | copy-start | bytes 1572868
  167.2 15.7 %copy-start.47 = (s32[1,512]{1,0:T(1,128)S(1)}, s32[1,512]{1,0:T(1,128)}, u32[]{:S(2)}) copy-start(s32[1,512]{1,0:T(1,128)} %get-tuple-element.120) | copy-start | bytes 6148
  212.9 106.4 %reduce-scatter.8.cloned.1.call-start = ((), (), s32[]{:S(2)}) async-start(), calls=%async_computation.9 | async-start | bytes 4718592 | tf_op jit(solution)/shard_map/reduce_scatter | solution.py:51
  218.9 175.0 %all-reduce.24.cloned.1.call-start = ((), (), s32[]{:S(2)}) async-start(), calls=%async_computation.15 | async-start | bytes 2097152
  266.6 72.2 %copy-start = (bf16[512,256]{1,0:T(8,128)(2,1)S(1)}, bf16[512,256]{1,0:T(8,128)(2,1)}, u32[]{:S(2)}) copy-start(bf16[512,256]{1,0:T(8,128)(2,1)} %convolution_convert_fusion.7) | copy-start | bytes 786436
  266.6 73.6 %copy-start.1 = (bf16[512,256]{1,0:T(8,128)(2,1)S(1)}, bf16[512,256]{1,0:T(8,128)(2,1)}, u32[]{:S(2)}) copy-start(bf16[512,256]{1,0:T(8,128)(2,1)} %convolution_convert_fusion.6) | copy-start | bytes 786436
  340.5 110.3 %copy-start.16 = (f32[2,512,64]{1,2,0:T(8,128)S(1)}, f32[2,512,64]{1,2,0:T(8,128)}, u32[]{:S(2)}) copy-start(f32[2,512,64]{1,2,0:T(8,128)} %param.25) | copy-start | bytes 786436
  342.0 108.8 %all-reduce.22.cloned.1.call-start = ((), (), s32[]{:S(2)}) async-start(), calls=%async_computation.13 | async-start | bytes 524288 | tf_op jit(solution)/shard_map/psum | solution.py:192
  395.7 146.8 %all-reduce.34.cloned.1.call-start = ((), (), s32[]{:S(2)}) async-start(), calls=%async_computation.20 | async-start | bytes 4194304 | tf_op jit(solution)/shard_map/psum | solution.py:93
  451.8 103.0 %copy-start.8 = (f32[2,512,64]{1,2,0:T(8,128)}, f32[2,512,64]{1,2,0:T(8,128)S(1)}, u32[]{:S(2)}) copy-start(f32[2,512,64]{1,2,0:T(8,128)S(1)} %multiply_add_fusion) | copy-start | bytes 786436
  455.9 190.3 %all-reduce.32.cloned.1.call-start = ((), (), s32[]{:S(2)}) async-start(), calls=%async_computation.19 | async-start | bytes 4194304 | tf_op jit(solution)/shard_map/psum | solution.py:93
  560.0 139.9 %reduce-scatter.14.cloned.1.call-start = ((), (), s32[]{:S(2)}) async-start(), calls=%async_computation.12 | async-start | bytes 4718592 | tf_op jit(solution)/shard_map/reduce_scatter | solution.py:51
  565.9 188.8 %reduce-scatter.10.cloned.1.call-start = ((), (), s32[]{:S(2)}) async-start(), calls=%async_computation.10 | async-start | bytes 4718592 | tf_op jit(solution)/shard_map/reduce_scatter | solution.py:51
  572.0 204.9 %reduce-scatter.16.cloned.1.call-start = ((), (), s32[]{:S(2)}) async-start(), calls=%async_computation.14 | async-start | bytes 163840
  655.5 103.7 %copy-start.36 = (f32[1,512]{1,0:T(1,128)S(1)}, f32[1,512]{1,0:T(1,128)}, u32[]{:S(2)}) copy-start(f32[1,512]{1,0:T(1,128)} %copy-done.35) | copy-start | bytes 6148
  655.5 103.7 %copy-start.46 = (f32[512]{0:T(512)S(1)}, f32[512]{0:T(512)}, u32[]{:S(2)}) copy-start(f32[512]{0:T(512)} %get-tuple-element.118) | copy-start | bytes 6148
  655.5 105.0 %copy-start.34 = (f32[1,512]{1,0:T(1,128)S(1)}, f32[1,512]{1,0:T(1,128)}, u32[]{:S(2)}) copy-start(f32[1,512]{1,0:T(1,128)} %copy-done.33) | copy-start | bytes 6148
  655.6 105.0 %copy-start.45 = (f32[512]{0:T(512)S(1)}, f32[512]{0:T(512)}, u32[]{:S(2)}) copy-start(f32[512]{0:T(512)} %get-tuple-element.119) | copy-start | bytes 6148
  655.6 106.2 %copy-start.69 = (f32[47]{0:T(128)S(1)}, f32[47]{0:T(128)}, u32[]{:S(2)}) copy-start(f32[47]{0:T(128)} %get-tuple-element.112) | copy-start | bytes 568
  655.6 106.2 %copy-start.70 = (f32[47]{0:T(128)S(1)}, f32[47]{0:T(128)}, u32[]{:S(2)}) copy-start(f32[47]{0:T(128)} %get-tuple-element.114) | copy-start | bytes 568
  655.6 106.2 %copy-start.60 = (f32[256]{0:T(256)S(1)}, f32[256]{0:T(256)}, u32[]{:S(2)}) copy-start(f32[256]{0:T(256)} %get-tuple-element.49) | copy-start | bytes 3076
  655.6 106.2 %copy-start.61 = (f32[256]{0:T(256)S(1)}, f32[256]{0:T(256)}, u32[]{:S(2)}) copy-start(f32[256]{0:T(256)} %get-tuple-element.58) | copy-start | bytes 3076
  655.6 106.2 %copy-start.62 = (f32[256]{0:T(256)S(1)}, f32[256]{0:T(256)}, u32[]{:S(2)}) copy-start(f32[256]{0:T(256)} %get-tuple-element.138) | copy-start | bytes 3076
  655.6 106.2 %copy-start.63 = (f32[256]{0:T(256)S(1)}, f32[256]{0:T(256)}, u32[]{:S(2)}) copy-start(f32[256]{0:T(256)} %get-tuple-element.141) | copy-start | bytes 3076
  655.6 106.2 %copy-start.14 = (f32[512,256]{1,0:T(8,128)S(1)}, f32[512,256]{1,0:T(8,128)}, u32[]{:S(2)}) copy-start(f32[512,256]{1,0:T(8,128)} %copy-done.13) | copy-start | bytes 1572868
  655.6 106.2 %copy-start.29 = (bf16[512,47]{0,1:T(8,128)(2,1)S(1)}, bf16[512,47]{0,1:T(8,128)(2,1)}, u32[]{:S(2)}) copy-start(bf16[512,47]{0,1:T(8,128)(2,1)} %copy-done.28) | copy-start | bytes 144388
  655.7 106.2 %copy-start.53 = (f32[256]{0:T(256)S(1)}, f32[256]{0:T(256)}, u32[]{:S(2)}) copy-start(f32[256]{0:T(256)} %copy-done.52) | copy-start | bytes 3076
  655.7 106.2 %copy-start.55 = (f32[256]{0:T(256)S(1)}, f32[256]{0:T(256)}, u32[]{:S(2)}) copy-start(f32[256]{0:T(256)} %copy-done.54) | copy-start | bytes 3076
  655.7 106.2 %copy-start.56 = (f32[1,1,256]{2,1,0:T(1,128)S(1)}, f32[1,1,256]{2,1,0:T(1,128)}, u32[]{:S(2)}) copy-start(f32[1,1,256]{2,1,0:T(1,128)} %get-tuple-element.125) | copy-start | bytes 3076
  655.7 106.2 %copy-start.68 = (f32[1,1,256]{2,1,0:T(1,128)S(1)}, f32[1,1,256]{2,1,0:T(1,128)}, u32[]{:S(2)}) copy-start(f32[1,1,256]{2,1,0:T(1,128)} %get-tuple-element.127) | copy-start | bytes 3076
  656.8 105.5 %copy-start.12 = (f32[512,256]{1,0:T(8,128)S(1)}, f32[512,256]{1,0:T(8,128)}, u32[]{:S(2)}) copy-start(f32[512,256]{1,0:T(8,128)} %copy-done.11) | copy-start | bytes 1572868
  656.8 105.5 %copy-start.24 = (bf16[512,47]{0,1:T(8,128)(2,1)S(1)}, bf16[512,47]{0,1:T(8,128)(2,1)}, u32[]{:S(2)}) copy-start(bf16[512,47]{0,1:T(8,128)(2,1)} %copy-done.23) | copy-start | bytes 144388
  656.9 105.5 %copy-start.49 = (f32[256]{0:T(256)S(1)}, f32[256]{0:T(256)}, u32[]{:S(2)}) copy-start(f32[256]{0:T(256)} %copy-done.48) | copy-start | bytes 3076
  656.9 105.5 %copy-start.51 = (f32[256]{0:T(256)S(1)}, f32[256]{0:T(256)}, u32[]{:S(2)}) copy-start(f32[256]{0:T(256)} %copy-done.50) | copy-start | bytes 3076
  756.3 45.6 %copy-start.32 = (f32[100,64]{0,1:T(8,128)S(1)}, f32[100,64]{0,1:T(8,128)}, u32[]{:S(2)}) copy-start(f32[100,64]{0,1:T(8,128)} %param.23) | copy-start | bytes 76804
  757.1 107.3 %all-reduce.30.cloned.1.call-start = ((), (), s32[]{:S(2)}) async-start(), calls=%async_computation.18 | async-start | bytes 4194304 | tf_op jit(solution)/shard_map/psum | solution.py:93
  759.2 208.2 %all-reduce.28.cloned.1.call-start = ((), (), s32[]{:S(2)}) async-start(), calls=%async_computation.17 | async-start | bytes 4194304 | tf_op jit(solution)/shard_map/psum | solution.py:93
  801.9 96.3 %copy-start.15 = (f32[100,64]{0,1:T(8,128)}, f32[100,64]{0,1:T(8,128)S(1)}, u32[]{:S(2)}) copy-start(f32[100,64]{0,1:T(8,128)S(1)} %multiply_add_fusion.2) | copy-start | bytes 76804
  876.8 194.4 %all-reduce.26.cloned.1.call-start = ((), (), s32[]{:S(2)}) async-start(), calls=%async_computation.16 | async-start | bytes 4194304 | tf_op jit(solution)/shard_map/psum | solution.py:93
  974.5 51.0 %copy-start.71 = (f32[47]{0:T(128)S(1)}, f32[47]{0:T(128)}, u32[]{:S(2)}) copy-start(f32[47]{0:T(128)} %param.29) | copy-start | bytes 568
  974.5 51.0 %copy-start.72 = (f32[47]{0:T(128)S(1)}, f32[47]{0:T(128)}, u32[]{:S(2)}) copy-start(f32[47]{0:T(128)} %param.30) | copy-start | bytes 568
  974.5 51.0 %copy-start.73 = (f32[47]{0:T(128)S(1)}, f32[47]{0:T(128)}, u32[]{:S(2)}) copy-start(f32[47]{0:T(128)} %param.31) | copy-start | bytes 568
  974.5 51.6 %copy-start.37 = (f32[2,2,256]{2,1,0:T(2,128)S(1)}, f32[2,2,256]{2,1,0:T(2,128)}, u32[]{:S(2)}) copy-start(f32[2,2,256]{2,1,0:T(2,128)} %param.32) | copy-start | bytes 12292
  974.5 51.6 %copy-start.57 = (f32[2,2,256]{2,1,0:T(2,128)S(1)}, f32[2,2,256]{2,1,0:T(2,128)}, u32[]{:S(2)}) copy-start(f32[2,2,256]{2,1,0:T(2,128)} %param.33) | copy-start | bytes 12292
  974.5 51.6 %copy-start.58 = (f32[2,2,256]{2,1,0:T(2,128)S(1)}, f32[2,2,256]{2,1,0:T(2,128)}, u32[]{:S(2)}) copy-start(f32[2,2,256]{2,1,0:T(2,128)} %param.34) | copy-start | bytes 12292
  974.6 52.4 %copy-start.27 = (f32[100,64]{0,1:T(8,128)S(1)}, f32[100,64]{0,1:T(8,128)}, u32[]{:S(2)}) copy-start(f32[100,64]{0,1:T(8,128)} %param.22) | copy-start | bytes 76804
  974.6 53.3 %copy-start.26 = (f32[256,47]{0,1:T(8,128)S(1)}, f32[256,47]{0,1:T(8,128)}, u32[]{:S(2)}) copy-start(f32[256,47]{0,1:T(8,128)} %param.26) | copy-start | bytes 144388
  974.6 53.2 %copy-start.30 = (f32[256,47]{0,1:T(8,128)S(1)}, f32[256,47]{0,1:T(8,128)}, u32[]{:S(2)}) copy-start(f32[256,47]{0,1:T(8,128)} %param.27) | copy-start | bytes 144388
  974.6 53.2 %copy-start.31 = (f32[256,47]{0,1:T(8,128)S(1)}, f32[256,47]{0,1:T(8,128)}, u32[]{:S(2)}) copy-start(f32[256,47]{0,1:T(8,128)} %param.28) | copy-start | bytes 144388
  (27 other events, 153.0 us)
Sparse Core Ops, SparseCore 0:
  25.4 28.9 all-gather.4
  56.9 27.8 all-gather.8
  104.1 28.0 all-gather.10
  133.9 28.0 all-gather.6
  213.1 51.3 reduce-scatter.11
  268.0 51.3 reduce-scatter.7
  342.1 51.7 all-reduce.23
  397.9 52.9 all-reduce.21
  456.0 86.4 all-reduce.33
  560.1 86.0 all-reduce.31
  649.5 50.2 reduce-scatter.13
  703.4 51.3 reduce-scatter.9
  757.6 19.1 reduce-scatter.15
  779.2 85.1 all-reduce.29
  876.9 90.3 all-reduce.27
  979.8 91.3 all-reduce.25
where the time goes:
time: 1100 us; the launch traced here: 1090 us
  waiting for transfers between devices  645 us (59%)
  blocking collectives  249 us (23%)
  matrix products  135 us (12%)
  other arithmetic  26.3 us (2%)
  between operations  20.5 us (2%)
    psum x5, waiting for transfers between devices, orthogonal_blocks(): lax.psum((gram_of(blocks[0]), gram_of(blocks[1]), gram_of(blocks[2])), 'g...  293 us
    reduce_scatter x4, waiting for transfers between devices, neighbour_back(): lax.psum_scatter(column_dot(adj, grads), 'node', scatter_dimension=0, til...  193 us
    psum x4, blocking collectives, orthogonal_blocks(): lax.psum((gram_of(blocks[0]), gram_of(blocks[1]), gram_of(blocks[2])), 'g...  78.2 us
    dot_general x45, matrix products, matmul_hi(): return jnp.dot(left, right, precision=lax.Precision.HIGHEST)  65.8 us
    unnamed x18, waiting for transfers between devices  65.4 us
    psum x1, waiting for transfers between devices, per_device(): lax.psum((grad_input, grad_conv_all, grad_head, grad_bias, grad_norm_all,...  55.1 us
    psum x1, blocking collectives, per_device(): count = lax.psum(jnp.sum(train_mask).astype(jnp.float32), ('grp', 'node'))  39.4 us
    all_gather x4, waiting for transfers between devices, neighbour_sum(): lax.all_gather(values, 'node', axis=0, tiled=True)  38.7 us
  transfers between devices with their start and end apart: 16, of which 15 were waited for; matrix products, arithmetic and copies ran while one was open for 6% of the time, Pallas kernels for 0%

commit v1 on v0

--- a/solution.py
+++ b/solution.py
@@ -1,6 +1,10 @@
+import functools
+
 import jax
 import jax.numpy as jnp
 from jax import lax
+from jax.experimental import pallas as pl
+from jax.experimental.pallas import tpu as pltpu
 from jax.sharding import PartitionSpec as P
 
 NS_STEPS = 5
@@ -234,6 +238,842 @@
         norm_second_new,
     )
 
+MESH = pl.DeviceIdType.MESH
+NT = (((1,), (1,)), ((), ()))
+NN = (((1,), (0,)), ((), ()))
+VMEM_BYTES = 56 * 1024 * 1024
+ROUNDS = 8
+
+
+def flip(index, bit):
+    return index + bit - 2 * bit * lax.rem(lax.div(index, bit), 2)
+
+
+def dot(left, right, dims=NN):
+    return lax.dot_general(left, right, dims, preferred_element_type=jnp.float32)
+
+
+def split(value):
+    high = lowered(value)
+    return high, lowered(value - high.astype(jnp.float32))
+
+
+def dot_three(left, right, dims=NN):
+    left_high, left_rest = left
+    right_high, right_rest = right
+    return (
+        dot(left_high, right_high, dims)
+        + dot(left_high, right_rest, dims)
+        + dot(left_rest, right_high, dims)
+    )
+
+
+def step_kernel(
+    groups,
+    classes,
+    feat,
+    adj,
+    labels,
+    train,
+    w_in,
+    m_in,
+    w_conv,
+    m_conv,
+    w_head,
+    f_head,
+    s_head,
+    w_bias,
+    f_bias,
+    s_bias,
+    w_norm,
+    f_norm,
+    s_norm,
+    o_small,
+    o_in,
+    o_in_m,
+    o_conv,
+    o_conv_m,
+    o_head,
+    o_head_f,
+    o_head_s,
+    o_norm,
+    o_norm_f,
+    o_norm_s,
+    av,
+    xg,
+    hg,
+    dg,
+    pad,
+    wt,
+    wt_in,
+    wn,
+    wt_head,
+    h0,
+    agg,
+    act,
+    slope,
+    ms,
+    axh,
+    accx,
+    acc,
+    h2,
+    dh,
+    dp,
+    gt,
+    q1,
+    q2,
+    ght,
+    st,
+    zs,
+    sums,
+    mpc,
+    mpi,
+    gbc,
+    gbi,
+    gbh,
+    rsc,
+    rsi,
+    rsh,
+    zc,
+    zi,
+    zh,
+    mf,
+    mfi,
+    hf,
+    y_conv,
+    y_in,
+    loc,
+    ga_s,
+    ga_r,
+    st_s,
+    st_r,
+    z_s,
+    z_r,
+    rs_s,
+    rs_r,
+    ag_s,
+    ag_r,
+):
+    f32 = jnp.float32
+    bf16 = jnp.bfloat16
+    graphs, rows, width = feat.shape
+    total = adj.shape[2]
+    hidden = w_head.shape[0]
+    wide = 2 * hidden
+    shard = hidden // groups
+    part = shard // 4
+    half = rows // 2
+    chunk = min(rows, 128)
+    chunks = rows // chunk
+    g = lax.axis_index("grp")
+    me = lax.axis_index("node")
+    core = lax.rem(me, 2)
+    chip = lax.div(me, 2)
+    n_sib, n_x, n_y, n_d = flip(me, 1), flip(me, 2), flip(me, 4), flip(flip(me, 2), 4)
+    peers = [
+        flip(flip(flip(me, 1) if b & 1 else me, 2) if b & 2 else (flip(me, 1) if b & 1 else me), 4)
+        if b & 4
+        else (flip(flip(me, 1) if b & 1 else me, 2) if b & 2 else flip(me, 1))
+        for b in range(1, 8)
+    ]
+    z_peers = [lax.rem(g + d, groups) for d in range(1, groups)]
+    z_from = [lax.rem(g + groups - d, groups) for d in range(1, groups)]
+    started = []
+
+    def send(src, dst, s_sem, r_sem, group, node):
+        copy = pltpu.make_async_remote_copy(
+            src_ref=src,
+            dst_ref=dst,
+            send_sem=s_sem,
+            recv_sem=r_sem,
+            device_id=(group, node),
+            device_id_type=MESH,
+        )
+        copy.start()
+        started.append(copy)
+        return copy
+
+    def lanes_of_core(span):
+        return pl.ds(pl.multiple_of(core * span, span), span)
+
+    barrier = pltpu.get_barrier_semaphore()
+    for node in peers:
+        pl.semaphore_signal(barrier, inc=1, device_id=(g, node), device_id_type=MESH)
+    for group in z_peers:
+        pl.semaphore_signal(barrier, inc=1, device_id=(group, me), device_id_type=MESH)
+
+    own_x = [pltpu.make_async_copy(feat.at[s], xg.at[s, me], loc.at[s]) for s in range(graphs)]
+    own_a = [pltpu.make_async_copy(adj.at[s], av.at[s], loc.at[graphs + s]) for s in range(graphs)]
+    for copy in own_x + own_a:
+        copy.start()
+
+    pad[...] = jnp.zeros_like(pad)
+
+    def transposed(value):
+        depth, span = value.shape
+        pad[pl.ds(0, depth), pl.ds(0, span)] = value
+        return pad[...].T
+
+    for l in range(2):
+        wt[l, pl.ds(pl.multiple_of(g * shard, shard), shard), :] = lowered(
+            transposed(w_conv[l])[:shard]
+        )
+    wt_in[pl.ds(pl.multiple_of(g * shard, shard), shard), :] = lowered(
+        transposed(w_in[...])[:shard, :width]
+    )
+    for copy in own_x:
+        copy.wait()
+    pl.semaphore_wait(barrier, 7 + groups - 1)
+
+    def gather_of(index, ref):
+        low, high = pl.ds(0, half), pl.ds(half, half)
+
+        def go(j, node, block, span=None):
+            view = ref.at[block] if span is None else ref.at[block, span]
+            return send(view, view, ga_s.at[index, j], ga_r.at[index, j], g, node)
+
+        kept = {}
+
+        def own():
+            kept[0] = go(0, n_x, me, low)
+            kept[1] = go(1, n_y, me, high)
+            kept[6] = go(6, n_sib, me)
+            kept[2] = go(2, n_x, me, high)
+            kept[3] = go(3, n_y, me, low)
+
+        def relay():
+            kept[0].wait_recv()
+            kept[4] = go(4, n_y, n_x, low)
+            kept[1].wait_recv()
+            kept[5] = go(5, n_x, n_y, high)
+
+        def near():
+            kept[2].wait_recv()
+            kept[7] = go(7, n_sib, n_x)
+            kept[3].wait_recv()
+            kept[8] = go(8, n_sib, n_y)
+
+        def far():
+            kept[4].wait_recv()
+            kept[5].wait_recv()
+            kept[9] = go(9, n_sib, n_d)
+
+        def near_ready():
+            for j in (6, 7, 8):
+                kept[j].wait_recv()
+
+        def far_ready():
+            kept[9].wait_recv()
+
+        return own, relay, near, far, near_ready, far_ready
+
+    def chip_at(i):
+        cx = lax.rem(lax.rem(chip, 2) + lax.rem(i, 2), 2)
+        cy = lax.rem(lax.div(chip, 2) + lax.div(i, 2), 2)
+        return cx + 2 * cy
+
+    def product(s, ref, out, first, last):
+        if first == 0:
+            out[...] = jnp.zeros_like(out)
+
+        def body(i, carry):
+            c = chip_at(i)
+            block = ref[pl.ds(2 * c, 2)].reshape(2 * rows, ref.shape[2])
+            left = av[s, :, pl.ds(pl.multiple_of(c * 2 * rows, 2 * rows), 2 * rows)]
+            out[...] += dot(left, block)
+            return carry
+
+        lax.fori_loop(first, last, body, 0)
+
+    def over_rows(body, carry):
+        def one(i, value):
+            return body(pl.ds(pl.multiple_of(i * chunk, chunk), chunk), value)
+
+        return lax.fori_loop(0, chunks, one, carry)
+
+    def fold(value):
+        return jnp.sum(value.reshape(chunk // 8, 8, hidden), 0)
+
+    st_copies = {}
+
+    def plane_send(k):
+        view = st.at[k, me]
+        st_copies[k] = [
+            send(view, view, st_s.at[k, i], st_r.at[k, i], g, node) for i, node in enumerate(peers)
+        ]
+
+    def plane_sum(k):
+        for copy in st_copies[k]:
+            copy.wait_recv()
+        value = st[k, 0]
+        for i in range(1, 8):
+            value = value + st[k, i]
+        return value
+
+    z_copies = {}
+
+    def z_send(k, view):
+        z_copies[k] = [
+            send(view, view, z_s.at[k, i], z_r.at[k, i], group, me)
+            for i, group in enumerate(z_peers)
+        ]
+
+    def z_wait(k):
+        for copy in z_copies[k]:
+            copy.wait_recv()
+
+    x_g = [gather_of(s, xg.at[s]) for s in range(2)]
+    h_g = [gather_of(2 + s, hg.at[s]) for s in range(2)]
+    d_g = [gather_of(4 + s, dg.at[s]) for s in range(2)]
+
+    x_g[0][0]()
+    own_rows = pl.ds(pl.multiple_of(g * shard, shard), shard)
+    z_send(0, wt_in.at[own_rows])
+    z_send(1, wt.at[0, own_rows])
+    z_send(2, wt.at[1, own_rows])
+    x_g[0][1]()
+    x_g[1][0]()
+    wt_head[...] = lowered(transposed(w_head[...])[:, :hidden])
+    bias_col = jnp.broadcast_to(w_bias[...], (8, classes))
+    pad[pl.ds(0, 8), pl.ds(0, classes)] = bias_col
+    bias_col = pad[pl.ds(0, 128), :].T[:64, :1]
+    for l in range(2):
+        piece = transposed(m_conv[l])[:shard].reshape(4, part, wide)
+        gt[0, pl.ds(0, shard), :] = piece.reshape(shard, wide)
+        rows_q = pl.ds(pl.multiple_of(chip * part, part), part)
+        mpc[l, g] = gt[0, rows_q, lanes_of_core(hidden)]
+    pad_in = transposed(m_in[...])[:shard, :width]
+    accx[pl.ds(0, shard), :] = pad_in
+    mpi[g] = accx[pl.ds(pl.multiple_of(chip * part, part), part), :]
+    z_send(6, mpc.at[0, g])
+    z_send(7, mpc.at[1, g])
+    z_send(8, mpi.at[g])
+    count_own = jnp.sum(train[...].astype(f32), axis=1, keepdims=True)
+    count_own = count_own[0:1] + count_own[1:2]
+
+    x_g[0][2]()
+    for copy in own_a:
+        copy.wait()
+
+    def forward_act(s, l, k, first, second, w_first, w_second):
+        acc[...] = dot(first, w_first) + dot(second, w_second)
+
+        def body(span, carry):
+            pre = acc[span, :]
+            square = pre * pre
+            inner = 0.7978845608028654 * pre * (1.0 + 0.044715 * square)
+            t = jnp.tanh(inner)
+            value = 0.5 * pre * (1.0 + t)
+            act[l, s, span, :] = value
+            slope[l, s, span, :] = 0.5 * (1.0 + t) + 0.5 * pre * (1.0 - t * t) * (
+                0.7978845608028654 * (1.0 + 3.0 * 0.044715 * square)
+            )
+            return carry[0] + fold(value), carry[1] + fold(value * value)
+
+        zero = jnp.zeros((8, hidden), f32)
+        one, two = over_rows(body, (zero, zero))
+        st[k, me] = jnp.zeros((8, hidden), f32)
+        st[k, me, 0:1, :] = jnp.sum(one, 0, keepdims=True)
+        st[k, me, 1:2, :] = jnp.sum(two, 0, keepdims=True)
+        if k == 0:
+            st[k, me, 2:3, :] = jnp.broadcast_to(count_own, (1, hidden))
+        plane_send(k)
+
+    def normalise(s, l, k, out):
+        sums_all = plane_sum(k)
+        mean = sums_all[0:1] / total
+        var = sums_all[1:2] / total - mean * mean
+        inv = lax.rsqrt(var + norm_eps)
+        ms[l, s, 0:1, :] = inv
+        gain, shift = w_norm[l, 0:1, :], w_norm[l, 1:2, :]
+
+        def body(span, carry):
+            normed = (act[l, s, span, :] - mean) * inv
+            act[l, s, span, :] = normed
+            out[span, :] = lowered(normed * gain + shift)
+            return carry
+
+        over_rows(body, 0)
+        return sums_all
+
+    def layer_zero(s):
+        high, rest = split(accx[...])
+        axh[s] = high
+        w = wt_in[...]
+        agg[0, s] = lowered(dot(high, w, NT) + dot(rest, w, NT))
+        h0[s] = lowered(dot(xg[s, me], w, NT))
+        forward_act(s, 0, s, h0[s], agg[0, s], wn[0, :hidden, :], wn[0, hidden:, :])
+
+    def layer_one(s):
+        agg[1, s] = lowered(acc[...])
+        forward_act(s, 1, 2 + s, hg[s, me], agg[1, s], wn[1, :hidden, :], wn[1, hidden:, :])
+
+    def head(s, count):
+        value = h2[s]
+        logits = dot(wt_head[pl.ds(0, 64), :], value, NT) + bias_col
+        at = lax.broadcasted_iota(jnp.int32, (64, rows), 0)
+        valid = at < classes
+        logits = jnp.where(valid, logits, -1e30)
+        shifted = logits - jnp.max(logits, 0, keepdims=True)
+        logp = shifted - jnp.log(jnp.sum(jnp.exp(shifted), 0, keepdims=True))
+        onehot = jnp.where(at == labels[s : s + 1, :], 1.0, 0.0)
+        target = jnp.where(valid, (1.0 - smoothing) * onehot + smoothing / classes, 0.0)
+        weights = train[s : s + 1, :].astype(f32)
+        node_loss = jnp.sum(target * logp, 0, keepdims=True)
+        loss = -jnp.sum(weights * node_loss, axis=1, keepdims=True)
+        delta = (weights / count) * (jnp.exp(logp) - target)
+        delta_low = lowered(delta)
+        value_t = dot(delta_low, value)
+        ght[...] = value_t if s == 0 else ght[...] + value_t
+        column = dot(jnp.ones((8, rows), bf16), delta_low, NT)
+        tall = jnp.concatenate([delta_low.astype(f32), jnp.zeros((64, rows), f32)], 0).T
+        dh[s] = lowered(dot(lowered(tall), wt_head[...])).astype(f32)
+        return loss, column
+
+    def backward_sums(s, l, k, extra=None):
+        def body(span, carry):
+            grad = dh[s, span, :]
+            return carry[0] + fold(grad), carry[1] + fold(grad * act[l, s, span, :])
+
+        zero = jnp.zeros((8, hidden), f32)
+        one, two = over_rows(body, (zero, zero))
+        st[k, me] = jnp.zeros((8, hidden), f32)
+        st[k, me, 0:1, :] = jnp.sum(one, 0, keepdims=True)
+        st[k, me, 1:2, :] = jnp.sum(two, 0, keepdims=True)
+        if extra is not None:
+            st[k, me, 2:3, 0:64] = extra[1][0:1]
+            st[k, me, 3:4, :] = jnp.broadcast_to(extra[0], (1, hidden))
+        plane_send(k)
+
+    def backward_pre(s, l, k):
+        sums_all = plane_sum(k)
+        sums[1 - l] = sums_all if s == 0 else sums[1 - l] + sums_all
+        gain = w_norm[l, 0:1, :]
+        inv = ms[l, s, 0:1, :]
+        first = gain * sums_all[0:1] / total
+        second = gain * sums_all[1:2] / total
+
+        def body(span, carry):
+            grad = dh[s, span, :] * gain - first - act[l, s, span, :] * second
+            dp[l, s, span, :] = lowered(grad * inv * slope[l, s, span, :])
+            return carry
+
+        over_rows(body, 0)
+
+    def conv_grads(s, l, left, right):
+        turned = dp[l, s].T
+        one, two = dot(turned, left), dot(turned, right)
+        if s == 0:
+            gt[l, :, :hidden] = one
+            gt[l, :, hidden:] = two
+        else:
+            gt[l, :, :hidden] += one
+            gt[l, :, hidden:] += two
+        return turned
+
+    rs_copies = {}
+
+    def pieces_send(k, src, dst, where):
+        rs_copies[k] = []
+        for i, node in enumerate(peers):
+            rs_copies[k].append(
+                send(where(src, node), dst.at[me], rs_s.at[k, i], rs_r.at[k, i], g, node)
+            )
+
+    def pieces_sum(k, src, dst, own):
+        dst[me] = own
+        for copy in rs_copies[k]:
+            copy.wait_recv()
+        value = dst[0].astype(f32)
+        for i in range(1, 8):
+            value = value + dst[i].astype(f32)
+        return value
+
+    def conv_piece(ref, node):
+        n_core, n_chip = lax.rem(node, 2), lax.div(node, 2)
+        return ref.at[:, n_chip, :, pl.ds(pl.multiple_of(n_core * hidden, hidden), hidden)]
+
+    def in_piece(ref, node):
+        return ref.at[:, lax.div(node, 2)]
+
+    def head_piece(ref, node):
+        n_core, n_chip = lax.rem(node, 2), lax.div(node, 2)
+        return ref.at[n_chip, :, pl.ds(pl.multiple_of(n_core * (hidden // 2), hidden // 2), hidden // 2)]
+
+    def over_z(k, buf):
+        z_wait(k)
+        value = buf[0].astype(f32)
+        for i in range(1, groups):
+            value = value + buf[i].astype(f32)
+        return value
+
+    ag_copies = {}
+
+    def spread(k, view, nodes):
+        ag_copies[k] = [
+            send(view, view, ag_s.at[k, i], ag_r.at[k, i], g, node) for i, node in nodes
+        ]
+
+    def spread_wait(k):
+        for copy in ag_copies[k]:
+            copy.wait_recv()
+
+    all_nodes = list(enumerate(peers))
+    same_core = [(i, peers[i]) for i in (1, 3, 5)]
+    core_lanes = lanes_of_core(hidden)
+    head_lanes = lanes_of_core(hidden // 2)
+
+    x_g[0][4]()
+    product(0, xg.at[0], accx, 0, 3)
+    x_g[1][1]()
+    x_g[0][3]()
+    x_g[0][5]()
+    product(0, xg.at[0], accx, 3, 4)
+    z_wait(0)
+    z_wait(1)
+    wn[0] = wt[0].T
+    layer_zero(0)
+    x_g[1][2]()
+    x_g[1][4]()
+    product(1, xg.at[1], accx, 0, 3)
+    x_g[1][3]()
+    x_g[1][5]()
+    product(1, xg.at[1], accx, 3, 4)
+    layer_zero(1)
+    count_plane = normalise(0, 0, 0, hg.at[0, me])
+    h_g[0][0]()
+    zs[0, g] = count_plane
+    z_send(3, zs.at[0, g])
+    z_wait(2)
+    wn[1] = wt[1].T
+    normalise(1, 0, 1, hg.at[1, me])
+    h_g[0][1]()
+    h_g[1][0]()
+    h_g[0][2]()
+    h_g[0][4]()
+    product(0, hg.at[0], acc, 0, 3)
+    h_g[0][3]()
+    h_g[1][1]()
+    h_g[0][5]()
+    product(0, hg.at[0], acc, 3, 4)
+    layer_one(0)
+    z_wait(3)
+    count = zs[0, 0]
+    for i in range(1, groups):
+        count = count + zs[0, i]
+    count = count[2:3, 0:1]
+    normalise(0, 1, 2, h2.at[0])
+    loss_row = head(0, count)
+    backward_sums(0, 1, 4, loss_row)
+    h_g[1][2]()
+    h_g[1][3]()
+    backward_pre(0, 1, 4)
+    dg[0, me] = lowered(dot(dp[1, 0], wt[1, :, hidden:]))
+    d_g[0][0]()
+    h_g[1][4]()
+    product(1, hg.at[1], acc, 0, 3)
+    h_g[1][5]()
+    product(1, hg.at[1], acc, 3, 4)
+    layer_one(1)
+    conv_grads(0, 1, hg[0, me], agg[1, 0])
+    dh[0] = dot(dp[1, 0], wt[1, :, :hidden])
+    normalise(1, 1, 3, h2.at[1])
+    loss_row = head(1, count)
+    backward_sums(1, 1, 5, loss_row)
+    d_g[0][1]()
+    backward_pre(1, 1, 5)
+    dg[1, me] = lowered(dot(dp[1, 1], wt[1, :, hidden:]))
+    d_g[1][0]()
+    conv_grads(1, 1, hg[1, me], agg[1, 1])
+    dh[1] = dot(dp[1, 1], wt[1, :, :hidden])
+    gbc[1] = lowered(gt[1]).reshape(groups, 4, part, wide)
+    gbh[...] = lowered(ght[...]).reshape(4, 16, hidden)
+    zs[1, g] = sums[0]
+    z_send(4, zs.at[1, g])
+    d_g[0][2]()
+    d_g[0][4]()
+    product(0, dg.at[0], acc, 0, 3)
+    d_g[0][3]()
+    d_g[1][1]()
+    d_g[0][5]()
+    product(0, dg.at[0], acc, 3, 4)
+    dh[0] = lowered(dh[0] + acc[...]).astype(f32)
+    backward_sums(0, 0, 6)
+    pieces_send(0, gbc.at[1], rsc.at[1], conv_piece)
+    pieces_send(1, gbh, rsh, head_piece)
+    d_g[1][2]()
+    d_g[1][4]()
+    product(1, dg.at[1], acc, 0, 3)
+    d_g[1][3]()
+    backward_pre(0, 0, 6)
+    turned = conv_grads(0, 0, h0[0], agg[0, 0])
+    q1[...] = dot(turned, xg[0, me])
+    q2[...] = dot(turned, axh[0])
+    d_g[1][5]()
+    product(1, dg.at[1], acc, 3, 4)
+    dh[1] = lowered(dh[1] + acc[...]).astype(f32)
+    backward_sums(1, 0, 7)
+    zc[1, g] = lowered(pieces_sum(0, None, rsc.at[1], conv_piece(gbc.at[1], me)[...]))
+    z_send(9, zc.at[1, g])
+    zh[g] = lowered(pieces_sum(1, None, rsh, head_piece(gbh, me)[...]))
+    z_send(10, zh.at[g])
+    backward_pre(1, 0, 7)
+    turned = conv_grads(1, 0, h0[1], agg[0, 1])
+    q1[...] += dot(turned, xg[1, me])
+    q2[...] += dot(turned, axh[1])
+    gbc[0] = lowered(gt[0]).reshape(groups, 4, part, wide)
+    pieces_send(2, gbc.at[0], rsc.at[0], conv_piece)
+    one, two = split(q1[...]), split(q2[...])
+    w_self, w_near = wn[0, :hidden, :], wn[0, hidden:, :]
+    g_in = dot(w_self, one[0]) + dot(w_self, one[1]) + dot(w_near, two[0]) + dot(w_near, two[1])
+    gbi[...] = lowered(g_in).reshape(groups, 4, part, width)
+    pieces_send(3, gbi, rsi, in_piece)
+    zs[2, g] = sums[1]
+    z_send(5, zs.at[2, g])
+
+    z_wait(7)
+    mf[1, :, chip, :, core_lanes] = muon_beta * mpc[1] + over_z(9, zc.at[1])
+    spread(0, mf.at[1, :, chip, :, core_lanes], all_nodes)
+    hf[chip, :, head_lanes] = over_z(10, zh)
+    spread(1, hf.at[chip, :, head_lanes], all_nodes)
+    zc[0, g] = lowered(pieces_sum(2, None, rsc.at[0], conv_piece(gbc.at[0], me)[...]))
+    z_send(11, zc.at[0, g])
+    zi[g] = lowered(pieces_sum(3, None, rsi, in_piece(gbi, me)[...]))
+    z_send(12, zi.at[g])
+    z_wait(6)
+    z_wait(8)
+    mf[0, :, chip, :, core_lanes] = muon_beta * mpc[0] + over_z(11, zc.at[0])
+    spread(2, mf.at[0, :, chip, :, core_lanes], all_nodes)
+    mfi[:, chip] = muon_beta * mpi[...] + over_z(12, zi)
+    spread(3, mfi.at[:, chip], same_core)
+
+    def scaled(value):
+        norm = jnp.sqrt(jnp.sum(jnp.sum(value * value, 0, keepdims=True), 1, keepdims=True))
+        return value / (norm + 1e-07)
+
+    def iterate(refs):
+        def body(i, carry):
+            for ref in refs:
+                value = ref[...]
+                pair = split(value)
+                gram = dot_three(pair, pair, NT)
+                gram_pair = split(gram)
+                poly = split(poly_second * gram + poly_third * dot_three(gram_pair, gram_pair))
+                ref[...] = poly_first * value + dot_three(poly, pair)
+            return carry
+
+        lax.fori_loop(0, NS_STEPS, body, 0)
+
+    def back(value):
+        depth, span = value.shape
+        flat = jnp.concatenate([value, jnp.zeros((128 - depth, span), f32)], 0)
+        return flat.T[:, :depth]
+
+    factor_conv = 0.2 * float(wide) ** 0.5
+    factor_in = 0.2 * float(max(width, hidden)) ** 0.5
+
+    def conv_out(l):
+        o_conv_m[l] = back(mf[l, g].reshape(shard, wide))
+        ortho = back(y_conv[l, own_rows, :])
+        weight = w_conv[l]
+        o_conv[l] = weight - muon_rate * (factor_conv * ortho + decay_rate * weight)
+
+    spread_wait(0)
+    y_conv[1] = scaled(mf[1].reshape(hidden, wide))
+    iterate([y_conv.at[1]])
+    conv_out(1)
+
+    def adam(weight, grad, first, second):
+        return adamw(weight, grad, first, second)
+
+    spread_wait(1)
+    grad = jnp.concatenate([hf[...].reshape(64, hidden), jnp.zeros((64, hidden), f32)], 0)
+    grad = grad.T[:, :classes]
+    o_head[...], o_head_f[...], o_head_s[...] = adam(w_head[...], grad, f_head[...], s_head[...])
+    z_wait(4)
+    z_wait(5)
+    late = zs[1, 0]
+    early = zs[2, 0]
+    for i in range(1, groups):
+        late = late + zs[1, i]
+        early = early + zs[2, i]
+    for l, rows_l in ((0, early), (1, late)):
+        grad = jnp.concatenate([rows_l[1:2], rows_l[0:1]], 0)
+        o_norm[l], o_norm_f[l], o_norm_s[l] = adam(w_norm[l], grad, f_norm[l], s_norm[l])
+    one, two, three = adam(w_bias[...], late[2:3, :classes], f_bias[...], s_bias[...])
+    o_small[...] = jnp.zeros_like(o_small)
+    o_small[0:1, 0:classes] = one
+    o_small[1:2, 0:classes] = two
+    o_small[2:3, 0:classes] = three
+    o_small[3:4, 0:1] = late[3:4, 0:1]
+    o_small[3:4, 1:2] = count
+
+    spread_wait(2)
+    spread_wait(3)
+    y_conv[0] = scaled(mf[0].reshape(hidden, wide))
+    y_in[...] = scaled(mfi[...].reshape(hidden, width))
+    iterate([y_conv.at[0], y_in])
+    conv_out(0)
+    pad[pl.ds(0, shard), pl.ds(0, width)] = mfi[g].reshape(shard, width)
+    o_in_m[...] = pad[pl.ds(0, 128), :].T[:width, :shard]
+    pad[pl.ds(0, shard), pl.ds(0, width)] = y_in[own_rows, :]
+    ortho = pad[pl.ds(0, 128), :].T[:width, :shard]
+    weight = w_in[...]
+    o_in[...] = weight - muon_rate * (factor_in * ortho + decay_rate * weight)
+    for copy in started:
+        copy.wait_send()
+
+
+def planned(mesh):
+    groups = mesh.shape["grp"]
+
+    def call(
+        features,
+        adjacency,
+        labels,
+        train_mask,
+        input_weight,
+        input_moment,
+        conv_weight,
+        conv_moment,
+        head_weight,
+        head_first,
+        head_second,
+        head_bias,
+        bias_first,
+        bias_second,
+        norm_params,
+        norm_first,
+        norm_second,
+    ):
+        f32, bf16 = jnp.float32, jnp.bfloat16
+        graphs, rows, width = features.shape
+        total = adjacency.shape[2]
+        hidden, classes = head_weight.shape
+        wide = 2 * hidden
+        shard = hidden // groups
+        part = shard // 4
+        vm = pltpu.VMEM
+        sem = pltpu.SemaphoreType.DMA
+        shape = jax.ShapeDtypeStruct
+        near = pl.BlockSpec(memory_space=pltpu.VMEM)
+        anywhere = pl.BlockSpec(memory_space=pl.ANY)
+        outs = pl.pallas_call(
+            functools.partial(step_kernel, groups, classes),
+            out_shape=[
+                shape((8, 128), f32),
+                shape(input_weight.shape, f32),
+                shape(input_weight.shape, f32),
+                shape(conv_weight.shape, f32),
+                shape(conv_weight.shape, f32),
+                shape(head_weight.shape, f32),
+                shape(head_weight.shape, f32),
+                shape(head_weight.shape, f32),
+                shape(norm_params.shape, f32),
+                shape(norm_params.shape, f32),
+                shape(norm_params.shape, f32),
+            ],
+            in_specs=[anywhere] * 2 + [near] * 15,
+            out_specs=[near] * 11,
+            scratch_shapes=[
+                vm((graphs, rows, total), bf16),
+                vm((graphs, 8, rows, width), bf16),
+                vm((graphs, 8, rows, hidden), bf16),
+                vm((graphs, 8, rows, hidden), bf16),
+                vm((wide, 128), f32),
+                vm((2, hidden, wide), bf16),
+                vm((hidden, width), bf16),
+                vm((2, wide, hidden), bf16),
+                vm((128, hidden), bf16),
+                vm((graphs, rows, hidden), bf16),
+                vm((2, graphs, rows, hidden), bf16),
+                vm((2, graphs, rows, hidden), f32),
+                vm((2, graphs, rows, hidden), f32),
+                vm((2, graphs, 8, hidden), f32),
+                vm((graphs, rows, width), bf16),
+                vm((rows, width), f32),
+                vm((rows, hidden), f32),
+                vm((graphs, rows, hidden), bf16),
+                vm((graphs, rows, hidden), f32),
+                vm((2, graphs, rows, hidden), bf16),
+                vm((2, hidden, wide), f32),
+                vm((hidden, width), f32),
+                vm((hidden, width), f32),
+                vm((64, hidden), f32),
+                vm((ROUNDS, 8, 8, hidden), f32),
+                vm((3, groups, 8, hidden), f32),
+                vm((2, 8, hidden), f32),
+                vm((2, groups, part, hidden), f32),
+                vm((groups, part, width), f32),
+                vm((2, groups, 4, part, wide), bf16),
+                vm((groups, 4, part, width), bf16),
+                vm((4, 16, hidden), bf16),
+                vm((2, 8, groups, part, hidden), bf16),
+                vm((8, groups, part, width), bf16),
+                vm((8, 16, hidden // 2), bf16),
+                vm((2, groups, groups, part, hidden), bf16),
+                vm((groups, groups, part, width), bf16),
+                vm((groups, 16, hidden // 2), bf16),
+                vm((2, groups, 4, part, wide), f32),
+                vm((groups, 4, part, width), f32),
+                vm((4, 16, hidden), f32),
+                vm((2, hidden, wide), f32),
+                vm((hidden, width), f32),
+                sem((2 * graphs,)),
+                sem((6, 10)),
+                sem((6, 10)),
+                sem((ROUNDS, 7)),
+                sem((ROUNDS, 7)),
+                sem((13, groups - 1)),
+                sem((13, groups - 1)),
+                sem((4, 7)),
+                sem((4, 7)),
+                sem((4, 7)),
+                sem((4, 7)),
+            ],
+            compiler_params=pltpu.CompilerParams(
+                collective_id=0, has_side_effects=True, vmem_limit_bytes=VMEM_BYTES
+            ),
+            name="train_step",
+        )(
+            features,
+            adjacency,
+            labels,
+            train_mask,
+            input_weight,
+            input_moment,
+            conv_weight,
+            conv_moment,
+            head_weight,
+            head_first,
+            head_second,
+            head_bias[None, :],
+            bias_first[None, :],
+            bias_second[None, :],
+            norm_params,
+            norm_first,
+            norm_second,
+        )
+        small, in_new, in_m, conv_new, conv_m, h_new, h_f, h_s, n_new, n_f, n_s = outs
+        return (
+            small[3, :2],
+            in_new,
+            in_m,
+            conv_new,
+            conv_m,
+            h_new,
+            h_f,
+            h_s,
+            small[0, :classes],
+            small[1, :classes],
+            small[2, :classes],
+            n_new,
+            n_f,
+            n_s,
+        )
+
+    return call
+
 
 def solution(mesh):
     placed = (
@@ -255,8 +1095,9 @@
         P(),
         P(),
     )
+    small = mesh.shape["node"] == 8 and mesh.shape["grp"] == 4
     return jax.shard_map(
-        per_device,
+        planned(mesh) if small else per_device,
         mesh=mesh,
         in_specs=placed,
         out_specs=(

time: 1100 us -> 148 us (0.13); the launches traced: 1090 us -> 148 us
  waiting for transfers between devices: 645 us -> 0 us
  blocking collectives: 249 us -> 0 us
  matrix products: 135 us -> 0 us
  Pallas kernels: 0 us -> 116 us
  other arithmetic: 26.3 us -> 0 us
  local copies, waits for them, and re-layouts: 10.3 us -> 31.3 us
  between operations: 20.5 us -> 0.66 us
    psum x6 -> x0, waiting for transfers between devices: 348 us -> none  [the longest x5 293 us: orthogonal_blocks(): lax.psum((gram_of(blocks[0]), gram_of(blocks[1]), gram_of(blocks[2])), 'g...]
    psum x11 -> x0, blocking collectives: 218 us -> none  [the longest x4 78.2 us: orthogonal_blocks(): lax.psum((gram_of(blocks[0]), gram_of(blocks[1]), gram_of(blocks[2])), 'g...]
    reduce_scatter x4 -> x0, waiting for transfers between devices: 193 us -> none  [neighbour_back(): lax.psum_scatter(column_dot(adj, grads), 'node', scatter_dimension=0, til...]
    dot_general x81 -> x0, matrix products: 135 us -> none  [the longest x45 65.8 us: matmul_hi(): return jnp.dot(left, right, precision=lax.Precision.HIGHEST)]
    pallas_call x0 -> x1, Pallas kernels: none -> 116 us  [call(): pl.pallas_call(functools.partial(step_kernel, groups, classes), out_shape...]
    unnamed x18 -> x0, waiting for transfers between devices: 65.4 us -> none
    all_gather x4 -> x0, waiting for transfers between devices: 38.7 us -> none  [neighbour_sum(): lax.all_gather(values, 'node', axis=0, tiled=True)]
    all_gather x2 -> x0, blocking collectives: 30.9 us -> none  [the longest x1 16 us: per_device(): lax.all_gather(lowered(conv_weight), 'grp', axis=2, tiled=True)]
  transfers between devices with their start and end apart: 16 -> 0, of which waited for: 15 -> 0; matrix products, arithmetic and copies ran while one was open for 6% -> 0% of each run, Pallas kernels for 0% -> 0%
where the time goes in v1:
time: 148 us
  Pallas kernels  116 us (78%)
  local copies, waits for them, and re-layouts  31.3 us (21%)
    pallas_call x1, Pallas kernels, call(): pl.pallas_call(functools.partial(step_kernel, groups, classes), out_shape...  116 us
    unnamed x18, local copies, waits for them, and re-layouts  28.8 us

profile of v1, /device:TPU:0, one launch (start us, length us, event | category | flops | bytes accessed | tf_op | source)
XLA Modules:
  0.0 147.5 jit_solution(10215919101187647442)
XLA Ops:
  0.6 1.5 copy.32.w_in
  2.1 1.5 copy.33.m_in
  3.6 1.6 %copy.36.w_head = f32[256,47]{1,0:T(8,128)} copy(f32[256,47]{0,1:T(8,128)} %param.25) | data formatting | bytes 96256 | tf_op args[8]
  5.1 1.6 %copy.37.f_head = f32[256,47]{1,0:T(8,128)} copy(f32[256,47]{0,1:T(8,128)} %param.26) | data formatting | bytes 96256 | tf_op args[9]
  6.7 1.6 %copy.38.s_head = f32[256,47]{1,0:T(8,128)} copy(f32[256,47]{0,1:T(8,128)} %param.27) | data formatting | bytes 96256 | tf_op args[10]
  8.3 1.8 %copy.31.feat = bf16[2,512,100]{2,1,0:T(8,128)(2,1)} copy(bf16[2,512,100]{1,0,2:T(2,128)(2,1)} %param.17) | data formatting | bytes 409600 | tf_op args[0]
  10.1 1.9 %copy.34.w_conv = f32[2,512,64]{2,1,0:T(8,128)} copy(f32[2,512,64]{1,2,0:T(8,128)} %param.23) | data formatting | bytes 524288 | tf_op args[6]
  12.0 1.9 %copy.35.m_conv = f32[2,512,64]{2,1,0:T(8,128)} copy(f32[2,512,64]{1,2,0:T(8,128)} %param.24) | data formatting | bytes 524288 | tf_op args[7]
  14.0 115.5 %train_step.1 = (f32[8,128]{1,0:T(8,128)}, f32[100,64]{1,0:T(8,128)}, f32[100,64]{1,0:T(8,128)}, f32[2,512,64]{2,1,0:T(8,128)}, f32[2,512,64]{2,1,0:T(8,128)}, /...) custom-call(bf16[2,512,100]{2,1,0:T(8,128)(2,1)} %copy.31.feat, ...), custom_call_target="tpu_custom_call" | custom-call | tf_op jit(solution)/shard_map/train_step/pallas_call | solution.py:961
  129.5 1.5 %copy.39 = f32[100,64]{0,1:T(8,128)} copy(f32[100,64]{1,0:T(8,128)} %get-tuple-element.37) | data formatting | bytes 51200
  131.0 1.2 slice_bitcast_fusion.3
  132.2 1.3 slice_bitcast_fusion
  133.5 1.5 %copy.40 = f32[100,64]{0,1:T(8,128)} copy(f32[100,64]{1,0:T(8,128)} %get-tuple-element.38) | data formatting | bytes 51200
  135.0 1.6 %copy.43 = f32[256,47]{0,1:T(8,128)} copy(f32[256,47]{1,0:T(8,128)} %get-tuple-element.41) | data formatting | bytes 96256
  136.6 1.6 %copy.44 = f32[256,47]{0,1:T(8,128)} copy(f32[256,47]{1,0:T(8,128)} %get-tuple-element.42) | data formatting | bytes 96256
  138.2 1.6 %copy.45 = f32[256,47]{0,1:T(8,128)} copy(f32[256,47]{1,0:T(8,128)} %get-tuple-element.43) | data formatting | bytes 96256
  139.8 1.9 %copy.41 = f32[2,512,64]{1,2,0:T(8,128)} copy(f32[2,512,64]{2,1,0:T(8,128)} %get-tuple-element.39) | data formatting | bytes 524288
  141.8 1.9 %copy.42 = f32[2,512,64]{1,2,0:T(8,128)} copy(f32[2,512,64]{2,1,0:T(8,128)} %get-tuple-element.40) | data formatting | bytes 524288
  143.7 1.3 copy.49
  145.0 1.3 copy.50
  146.2 1.3 copy.51

commit v2 on v1

--- a/solution.py
+++ b/solution.py
@@ -261,10 +261,11 @@
 def dot_three(left, right, dims=NN):
     left_high, left_rest = left
     right_high, right_rest = right
-    return (
-        dot(left_high, right_high, dims)
-        + dot(left_high, right_rest, dims)
-        + dot(left_rest, right_high, dims)
+    axis = dims[0][1][0]
+    return dot(
+        jnp.concatenate([left_high, left_high, left_rest], 1),
+        jnp.concatenate([right_high, right_rest, right_high], axis),
+        dims,
     )
 
 
@@ -288,7 +289,7 @@
     w_norm,
     f_norm,
     s_norm,
-    o_small,
+    o_loss,
     o_in,
     o_in_m,
     o_conv,
@@ -296,6 +297,9 @@
     o_head,
     o_head_f,
     o_head_s,
+    o_bias,
+    o_bias_f,
+    o_bias_s,
     o_norm,
     o_norm_f,
     o_norm_s,
@@ -304,8 +308,9 @@
     hg,
     dg,
     pad,
-    wt,
-    wt_in,
+    padh,
+    wa,
+    wb,
     wn,
     wt_head,
     h0,
@@ -322,12 +327,14 @@
     gt,
     q1,
     q2,
+    tall_in,
     ght,
     st,
     zs,
     sums,
     mpc,
-    mpi,
+    mit,
+    mi,
     gbc,
     gbi,
     gbh,
@@ -349,6 +356,8 @@
     st_r,
     z_s,
     z_r,
+    zf_s,
+    zf_r,
     rs_s,
     rs_r,
     ag_s,
@@ -356,13 +365,14 @@
 ):
     f32 = jnp.float32
     bf16 = jnp.bfloat16
-    graphs, rows, width = feat.shape
+    width, graphs, rows = feat.shape
     total = adj.shape[2]
-    hidden = w_head.shape[0]
+    hidden = w_head.shape[1]
     wide = 2 * hidden
     shard = hidden // groups
     part = shard // 4
     half = rows // 2
+    span_in = 16 * ((width + 15) // 16)
     chunk = min(rows, 128)
     chunks = rows // chunk
     g = lax.axis_index("grp")
@@ -370,12 +380,7 @@
     core = lax.rem(me, 2)
     chip = lax.div(me, 2)
     n_sib, n_x, n_y, n_d = flip(me, 1), flip(me, 2), flip(me, 4), flip(flip(me, 2), 4)
-    peers = [
-        flip(flip(flip(me, 1) if b & 1 else me, 2) if b & 2 else (flip(me, 1) if b & 1 else me), 4)
-        if b & 4
-        else (flip(flip(me, 1) if b & 1 else me, 2) if b & 2 else flip(me, 1))
-        for b in range(1, 8)
-    ]
+    peers = [n_d, flip(n_d, 1), n_x, n_y, flip(n_x, 1), flip(n_y, 1), n_sib]
     z_peers = [lax.rem(g + d, groups) for d in range(1, groups)]
     z_from = [lax.rem(g + groups - d, groups) for d in range(1, groups)]
     started = []
@@ -402,34 +407,35 @@
     for group in z_peers:
         pl.semaphore_signal(barrier, inc=1, device_id=(group, me), device_id_type=MESH)
 
-    own_x = [pltpu.make_async_copy(feat.at[s], xg.at[s, me], loc.at[s]) for s in range(graphs)]
-    own_a = [pltpu.make_async_copy(adj.at[s], av.at[s], loc.at[graphs + s]) for s in range(graphs)]
-    for copy in own_x + own_a:
+    own_a = [pltpu.make_async_copy(adj.at[s], av.at[s], loc.at[s]) for s in range(graphs)]
+    part_rows = pl.ds(pl.multiple_of(chip * part, part), part)
+    core_lanes = lanes_of_core(hidden)
+    own_m = [
+        pltpu.make_async_copy(m_conv.at[l, part_rows, core_lanes], mpc.at[l, g], loc.at[graphs + l])
+        for l in range(2)
+    ]
+    for copy in own_a + own_m:
         copy.start()
 
-    pad[...] = jnp.zeros_like(pad)
-
-    def transposed(value):
-        depth, span = value.shape
-        pad[pl.ds(0, depth), pl.ds(0, span)] = value
-        return pad[...].T
-
-    for l in range(2):
-        wt[l, pl.ds(pl.multiple_of(g * shard, shard), shard), :] = lowered(
-            transposed(w_conv[l])[:shard]
-        )
-    wt_in[pl.ds(pl.multiple_of(g * shard, shard), shard), :] = lowered(
-        transposed(w_in[...])[:shard, :width]
-    )
-    for copy in own_x:
-        copy.wait()
+    high_rows = pl.ds(pl.multiple_of(g * shard, shard), shard)
+    padh[...] = jnp.zeros_like(padh)
+    for s in range(graphs):
+        padh[pl.ds(0, width), :] = feat[:, s, :].astype(f32)
+        xg[s, me] = lowered(padh[pl.ds(0, span_in), :])
+    mit[...] = jnp.zeros_like(mit)
+    mit[high_rows, pl.ds(0, width)] = w_in[...]
+    wa[high_rows, pl.ds(0, wide)] = lowered(w_conv[0])
+    wa[high_rows, pl.ds(wide, 128)] = lowered(mit[high_rows, :])
+    wb[high_rows, :] = lowered(w_conv[1])
     pl.semaphore_wait(barrier, 7 + groups - 1)
 
-    def gather_of(index, ref):
+    def gather_of(index, ref, by_lane=False):
         low, high = pl.ds(0, half), pl.ds(half, half)
 
         def go(j, node, block, span=None):
-            view = ref.at[block] if span is None else ref.at[block, span]
+            view = ref.at[block]
+            if span is not None:
+                view = ref.at[block, :, span] if by_lane else ref.at[block, span]
             return send(view, view, ga_s.at[index, j], ga_r.at[index, j], g, node)
 
         kept = {}
@@ -484,6 +490,18 @@
             return carry
 
         lax.fori_loop(first, last, body, 0)
+
+    def product_x(s, first, last):
+        if first == 0:
+            accx[...] = jnp.zeros_like(accx)
+
+        def body(i, carry):
+            block = 2 * chip_at(lax.div(i, 2)) + lax.rem(i, 2)
+            left = av[s, :, pl.ds(pl.multiple_of(block * rows, rows), rows)]
+            accx[...] += dot(left, xg[s, block], NT)
+            return carry
+
+        lax.fori_loop(2 * first, 2 * last, body, 0)
 
     def over_rows(body, carry):
         def one(i, value):
@@ -522,36 +540,46 @@
         for copy in z_copies[k]:
             copy.wait_recv()
 
-    x_g = [gather_of(s, xg.at[s]) for s in range(2)]
+    x_g = [gather_of(s, xg.at[s], True) for s in range(2)]
     h_g = [gather_of(2 + s, hg.at[s]) for s in range(2)]
     d_g = [gather_of(4 + s, dg.at[s]) for s in range(2)]
 
+    own_rows = pl.ds(pl.multiple_of(g * shard, shard), shard)
+    strip = shard // 2
+
+    def strip_of(group):
+        return pl.ds(pl.multiple_of(group * shard + core * strip, strip), strip)
+
+    forwards = {}
+
+    def z_forward(k, ref):
+        forwards[k] = []
+        for i, group in enumerate(z_from):
+            z_copies[k][i].wait_recv()
+            view = ref.at[strip_of(group)]
+            forwards[k].append(send(view, view, zf_s.at[k, i], zf_r.at[k, i], g, n_sib))
+
+    def z_forwarded(k):
+        for copy in forwards[k]:
+            copy.wait_recv()
+
     x_g[0][0]()
-    own_rows = pl.ds(pl.multiple_of(g * shard, shard), shard)
-    z_send(0, wt_in.at[own_rows])
-    z_send(1, wt.at[0, own_rows])
-    z_send(2, wt.at[1, own_rows])
+    z_send(0, wa.at[strip_of(g)])
+    mit[high_rows, pl.ds(0, width)] = m_in[...]
     x_g[0][1]()
     x_g[1][0]()
-    wt_head[...] = lowered(transposed(w_head[...])[:, :hidden])
-    bias_col = jnp.broadcast_to(w_bias[...], (8, classes))
-    pad[pl.ds(0, 8), pl.ds(0, classes)] = bias_col
-    bias_col = pad[pl.ds(0, 128), :].T[:64, :1]
-    for l in range(2):
-        piece = transposed(m_conv[l])[:shard].reshape(4, part, wide)
-        gt[0, pl.ds(0, shard), :] = piece.reshape(shard, wide)
-        rows_q = pl.ds(pl.multiple_of(chip * part, part), part)
-        mpc[l, g] = gt[0, rows_q, lanes_of_core(hidden)]
-    pad_in = transposed(m_in[...])[:shard, :width]
-    accx[pl.ds(0, shard), :] = pad_in
-    mpi[g] = accx[pl.ds(pl.multiple_of(chip * part, part), part), :]
-    z_send(6, mpc.at[0, g])
-    z_send(7, mpc.at[1, g])
-    z_send(8, mpi.at[g])
+    z_send(1, wb.at[strip_of(g)])
+    padh[...] = jnp.zeros_like(padh)
+    padh[pl.ds(0, classes), pl.ds(0, hidden)] = w_head[...]
+    wt_head[...] = lowered(padh[:, :hidden])
+    pad[...] = jnp.zeros_like(pad)
+    pad[pl.ds(0, 8), pl.ds(0, classes)] = jnp.broadcast_to(w_bias[...], (8, classes))
+    bias_col = pad[...].T[:64, :1]
     count_own = jnp.sum(train[...].astype(f32), axis=1, keepdims=True)
     count_own = count_own[0:1] + count_own[1:2]
-
     x_g[0][2]()
+    for copy in own_m:
+        copy.wait()
     for copy in own_a:
         copy.wait()
 
@@ -599,9 +627,9 @@
     def layer_zero(s):
         high, rest = split(accx[...])
         axh[s] = high
-        w = wt_in[...]
+        w = wa[:, wide : wide + span_in]
         agg[0, s] = lowered(dot(high, w, NT) + dot(rest, w, NT))
-        h0[s] = lowered(dot(xg[s, me], w, NT))
+        h0[s] = lowered(dot(xg[s, me].T, w, NT))
         forward_act(s, 0, s, h0[s], agg[0, s], wn[0, :hidden, :], wn[0, hidden:, :])
 
     def layer_one(s):
@@ -694,7 +722,7 @@
         return ref.at[:, n_chip, :, pl.ds(pl.multiple_of(n_core * hidden, hidden), hidden)]
 
     def in_piece(ref, node):
-        return ref.at[:, lax.div(node, 2)]
+        return ref.at[node]
 
     def head_piece(ref, node):
         n_core, n_chip = lax.rem(node, 2), lax.div(node, 2)
@@ -709,46 +737,57 @@
 
     ag_copies = {}
 
-    def spread(k, view, nodes):
+    def spread(k, view_of):
+        view = view_of(me)
         ag_copies[k] = [
-            send(view, view, ag_s.at[k, i], ag_r.at[k, i], g, node) for i, node in nodes
+            send(view, view, ag_s.at[k, i], ag_r.at[k, i], g, node)
+            for i, node in enumerate((n_d, n_x, n_y, n_sib))
         ]
 
+    def spread_forward(k, view_of):
+        for i, node in ((1, n_x), (2, n_y), (0, n_d)):
+            ag_copies[k][i].wait_recv()
+            view = view_of(node)
+            ag_copies[k].append(
+                send(view, view, ag_s.at[k, 4 + i], ag_r.at[k, 4 + i], g, n_sib)
+            )
+
     def spread_wait(k):
-        for copy in ag_copies[k]:
+        for copy in ag_copies[k][3:]:
             copy.wait_recv()
 
-    all_nodes = list(enumerate(peers))
-    same_core = [(i, peers[i]) for i in (1, 3, 5)]
-    core_lanes = lanes_of_core(hidden)
     head_lanes = lanes_of_core(hidden // 2)
 
     x_g[0][4]()
-    product(0, xg.at[0], accx, 0, 3)
+    product_x(0, 0, 3)
     x_g[1][1]()
     x_g[0][3]()
+    z_forward(0, wa)
     x_g[0][5]()
-    product(0, xg.at[0], accx, 3, 4)
-    z_wait(0)
-    z_wait(1)
-    wn[0] = wt[0].T
+    product_x(0, 3, 4)
+    z_forwarded(0)
+    wn[0] = wa[:, :wide].T
     layer_zero(0)
     x_g[1][2]()
     x_g[1][4]()
-    product(1, xg.at[1], accx, 0, 3)
+    product_x(1, 0, 3)
     x_g[1][3]()
     x_g[1][5]()
-    product(1, xg.at[1], accx, 3, 4)
+    product_x(1, 3, 4)
     layer_zero(1)
     count_plane = normalise(0, 0, 0, hg.at[0, me])
     h_g[0][0]()
     zs[0, g] = count_plane
     z_send(3, zs.at[0, g])
-    z_wait(2)
-    wn[1] = wt[1].T
+    z_forward(1, wb)
     normalise(1, 0, 1, hg.at[1, me])
     h_g[0][1]()
     h_g[1][0]()
+    z_send(6, mpc.at[0, g])
+    z_send(7, mpc.at[1, g])
+    z_send(8, mit.at[own_rows])
+    z_forwarded(1)
+    wn[1] = wb[...].T
     h_g[0][2]()
     h_g[0][4]()
     product(0, hg.at[0], acc, 0, 3)
@@ -768,7 +807,7 @@
     h_g[1][2]()
     h_g[1][3]()
     backward_pre(0, 1, 4)
-    dg[0, me] = lowered(dot(dp[1, 0], wt[1, :, hidden:]))
+    dg[0, me] = lowered(dot(dp[1, 0], wb[:, hidden:]))
     d_g[0][0]()
     h_g[1][4]()
     product(1, hg.at[1], acc, 0, 3)
@@ -776,16 +815,16 @@
     product(1, hg.at[1], acc, 3, 4)
     layer_one(1)
     conv_grads(0, 1, hg[0, me], agg[1, 0])
-    dh[0] = dot(dp[1, 0], wt[1, :, :hidden])
+    dh[0] = dot(dp[1, 0], wb[:, :hidden])
     normalise(1, 1, 3, h2.at[1])
     loss_row = head(1, count)
     backward_sums(1, 1, 5, loss_row)
     d_g[0][1]()
     backward_pre(1, 1, 5)
-    dg[1, me] = lowered(dot(dp[1, 1], wt[1, :, hidden:]))
+    dg[1, me] = lowered(dot(dp[1, 1], wb[:, hidden:]))
     d_g[1][0]()
     conv_grads(1, 1, hg[1, me], agg[1, 1])
-    dh[1] = dot(dp[1, 1], wt[1, :, :hidden])
+    dh[1] = dot(dp[1, 1], wb[:, :hidden])
     gbc[1] = lowered(gt[1]).reshape(groups, 4, part, wide)
     gbh[...] = lowered(ght[...]).reshape(4, 16, hidden)
     zs[1, g] = sums[0]
@@ -807,7 +846,7 @@
     d_g[1][3]()
     backward_pre(0, 0, 6)
     turned = conv_grads(0, 0, h0[0], agg[0, 0])
-    q1[...] = dot(turned, xg[0, me])
+    q1[...] = dot(turned, xg[0, me], NT)
     q2[...] = dot(turned, axh[0])
     d_g[1][5]()
     product(1, dg.at[1], acc, 3, 4)
@@ -819,33 +858,47 @@
     z_send(10, zh.at[g])
     backward_pre(1, 0, 7)
     turned = conv_grads(1, 0, h0[1], agg[0, 1])
-    q1[...] += dot(turned, xg[1, me])
+    q1[...] += dot(turned, xg[1, me], NT)
     q2[...] += dot(turned, axh[1])
     gbc[0] = lowered(gt[0]).reshape(groups, 4, part, wide)
     pieces_send(2, gbc.at[0], rsc.at[0], conv_piece)
     one, two = split(q1[...]), split(q2[...])
     w_self, w_near = wn[0, :hidden, :], wn[0, hidden:, :]
     g_in = dot(w_self, one[0]) + dot(w_self, one[1]) + dot(w_near, two[0]) + dot(w_near, two[1])
-    gbi[...] = lowered(g_in).reshape(groups, 4, part, width)
+    tall_in[:, pl.ds(0, span_in)] = g_in
+    gbi[...] = lowered(tall_in[...].T).reshape(8, 16, hidden)
     pieces_send(3, gbi, rsi, in_piece)
     zs[2, g] = sums[1]
     z_send(5, zs.at[2, g])
 
+    def conv_view(l):
+        return lambda node: conv_piece(mf.at[l], node)
+
+    def head_view(node):
+        return head_piece(hf, node)
+
+    def in_view(node):
+        return mfi.at[node]
+
     z_wait(7)
     mf[1, :, chip, :, core_lanes] = muon_beta * mpc[1] + over_z(9, zc.at[1])
-    spread(0, mf.at[1, :, chip, :, core_lanes], all_nodes)
+    spread(0, conv_view(1))
     hf[chip, :, head_lanes] = over_z(10, zh)
-    spread(1, hf.at[chip, :, head_lanes], all_nodes)
+    spread(1, head_view)
+    z_wait(6)
+    z_wait(8)
+    tall_in[...] = mit[...]
+    mi[...] = tall_in[...].T.reshape(8, 16, hidden)
     zc[0, g] = lowered(pieces_sum(2, None, rsc.at[0], conv_piece(gbc.at[0], me)[...]))
     z_send(11, zc.at[0, g])
-    zi[g] = lowered(pieces_sum(3, None, rsi, in_piece(gbi, me)[...]))
+    zi[g] = lowered(pieces_sum(3, None, rsi, gbi[me]))
     z_send(12, zi.at[g])
-    z_wait(6)
-    z_wait(8)
+    spread_forward(0, conv_view(1))
+    spread_forward(1, head_view)
     mf[0, :, chip, :, core_lanes] = muon_beta * mpc[0] + over_z(11, zc.at[0])
-    spread(2, mf.at[0, :, chip, :, core_lanes], all_nodes)
-    mfi[:, chip] = muon_beta * mpi[...] + over_z(12, zi)
-    spread(3, mfi.at[:, chip], same_core)
+    spread(2, conv_view(0))
+    mfi[me] = muon_beta * mi[me] + over_z(12, zi)
+    spread(3, in_view)
 
     def scaled(value):
         norm = jnp.sqrt(jnp.sum(jnp.sum(value * value, 0, keepdims=True), 1, keepdims=True))
@@ -864,31 +917,27 @@
 
         lax.fori_loop(0, NS_STEPS, body, 0)
 
-    def back(value):
-        depth, span = value.shape
-        flat = jnp.concatenate([value, jnp.zeros((128 - depth, span), f32)], 0)
-        return flat.T[:, :depth]
-
     factor_conv = 0.2 * float(wide) ** 0.5
     factor_in = 0.2 * float(max(width, hidden)) ** 0.5
 
     def conv_out(l):
-        o_conv_m[l] = back(mf[l, g].reshape(shard, wide))
-        ortho = back(y_conv[l, own_rows, :])
+        o_conv_m[l] = mf[l, g].reshape(shard, wide)
+        ortho = y_conv[l, own_rows, :]
         weight = w_conv[l]
         o_conv[l] = weight - muon_rate * (factor_conv * ortho + decay_rate * weight)
 
     spread_wait(0)
     y_conv[1] = scaled(mf[1].reshape(hidden, wide))
     iterate([y_conv.at[1]])
+    spread_forward(2, conv_view(0))
+    spread_forward(3, in_view)
     conv_out(1)
 
     def adam(weight, grad, first, second):
         return adamw(weight, grad, first, second)
 
     spread_wait(1)
-    grad = jnp.concatenate([hf[...].reshape(64, hidden), jnp.zeros((64, hidden), f32)], 0)
-    grad = grad.T[:, :classes]
+    grad = hf[...].reshape(64, hidden)[:classes]
     o_head[...], o_head_f[...], o_head_s[...] = adam(w_head[...], grad, f_head[...], s_head[...])
     z_wait(4)
     z_wait(5)
@@ -900,24 +949,21 @@
     for l, rows_l in ((0, early), (1, late)):
         grad = jnp.concatenate([rows_l[1:2], rows_l[0:1]], 0)
         o_norm[l], o_norm_f[l], o_norm_s[l] = adam(w_norm[l], grad, f_norm[l], s_norm[l])
-    one, two, three = adam(w_bias[...], late[2:3, :classes], f_bias[...], s_bias[...])
-    o_small[...] = jnp.zeros_like(o_small)
-    o_small[0:1, 0:classes] = one
-    o_small[1:2, 0:classes] = two
-    o_small[2:3, 0:classes] = three
-    o_small[3:4, 0:1] = late[3:4, 0:1]
-    o_small[3:4, 1:2] = count
+    o_bias[...], o_bias_f[...], o_bias_s[...] = adam(
+        w_bias[...], late[2:3, :classes], f_bias[...], s_bias[...]
+    )
+    o_loss[...] = jnp.concatenate([late[3:4, 0:1], count], 1)
 
     spread_wait(2)
     spread_wait(3)
     y_conv[0] = scaled(mf[0].reshape(hidden, wide))
-    y_in[...] = scaled(mfi[...].reshape(hidden, width))
+    y_in[...] = scaled(mfi[...].reshape(128, hidden))
     iterate([y_conv.at[0], y_in])
     conv_out(0)
-    pad[pl.ds(0, shard), pl.ds(0, width)] = mfi[g].reshape(shard, width)
-    o_in_m[...] = pad[pl.ds(0, 128), :].T[:width, :shard]
-    pad[pl.ds(0, shard), pl.ds(0, width)] = y_in[own_rows, :]
-    ortho = pad[pl.ds(0, 128), :].T[:width, :shard]
+    tall_in[...] = mfi[...].reshape(128, hidden).T
+    o_in_m[...] = tall_in[own_rows, :][:, :width]
+    tall_in[...] = y_in[...].T
+    ortho = tall_in[own_rows, :][:, :width]
     weight = w_in[...]
     o_in[...] = weight - muon_rate * (factor_in * ortho + decay_rate * weight)
     for copy in started:
@@ -953,36 +999,42 @@
         wide = 2 * hidden
         shard = hidden // groups
         part = shard // 4
+        span_in = 16 * ((width + 15) // 16)
         vm = pltpu.VMEM
         sem = pltpu.SemaphoreType.DMA
         shape = jax.ShapeDtypeStruct
         near = pl.BlockSpec(memory_space=pltpu.VMEM)
         anywhere = pl.BlockSpec(memory_space=pl.ANY)
+        results = [
+            shape((1, 2), f32),
+            shape((shard, width), f32),
+            shape((shard, width), f32),
+            shape((2, shard, wide), f32),
+            shape((2, shard, wide), f32),
+            shape((classes, hidden), f32),
+            shape((classes, hidden), f32),
+            shape((classes, hidden), f32),
+            shape((1, classes), f32),
+            shape((1, classes), f32),
+            shape((1, classes), f32),
+            shape(norm_params.shape, f32),
+            shape(norm_params.shape, f32),
+            shape(norm_params.shape, f32),
+        ]
         outs = pl.pallas_call(
             functools.partial(step_kernel, groups, classes),
-            out_shape=[
-                shape((8, 128), f32),
-                shape(input_weight.shape, f32),
-                shape(input_weight.shape, f32),
-                shape(conv_weight.shape, f32),
-                shape(conv_weight.shape, f32),
-                shape(head_weight.shape, f32),
-                shape(head_weight.shape, f32),
-                shape(head_weight.shape, f32),
-                shape(norm_params.shape, f32),
-                shape(norm_params.shape, f32),
-                shape(norm_params.shape, f32),
-            ],
-            in_specs=[anywhere] * 2 + [near] * 15,
-            out_specs=[near] * 11,
+            out_shape=results,
+            in_specs=[near, anywhere, near, near, near, near, near, anywhere] + [near] * 9,
+            out_specs=[near] * 14,
             scratch_shapes=[
                 vm((graphs, rows, total), bf16),
-                vm((graphs, 8, rows, width), bf16),
+                vm((graphs, 8, span_in, rows), bf16),
                 vm((graphs, 8, rows, hidden), bf16),
                 vm((graphs, 8, rows, hidden), bf16),
-                vm((wide, 128), f32),
-                vm((2, hidden, wide), bf16),
-                vm((hidden, width), bf16),
+                vm((128, 128), f32),
+                vm((128, rows), f32),
+                vm((hidden, wide + 128), bf16),
+                vm((hidden, wide), bf16),
                 vm((2, wide, hidden), bf16),
                 vm((128, hidden), bf16),
                 vm((graphs, rows, hidden), bf16),
@@ -990,42 +1042,46 @@
                 vm((2, graphs, rows, hidden), f32),
                 vm((2, graphs, rows, hidden), f32),
                 vm((2, graphs, 8, hidden), f32),
-                vm((graphs, rows, width), bf16),
-                vm((rows, width), f32),
+                vm((graphs, rows, span_in), bf16),
+                vm((rows, span_in), f32),
                 vm((rows, hidden), f32),
                 vm((graphs, rows, hidden), bf16),
                 vm((graphs, rows, hidden), f32),
                 vm((2, graphs, rows, hidden), bf16),
                 vm((2, hidden, wide), f32),
-                vm((hidden, width), f32),
-                vm((hidden, width), f32),
+                vm((hidden, span_in), f32),
+                vm((hidden, span_in), f32),
+                vm((hidden, 128), f32),
                 vm((64, hidden), f32),
                 vm((ROUNDS, 8, 8, hidden), f32),
                 vm((3, groups, 8, hidden), f32),
                 vm((2, 8, hidden), f32),
                 vm((2, groups, part, hidden), f32),
-                vm((groups, part, width), f32),
+                vm((hidden, 128), f32),
+                vm((8, 16, hidden), f32),
                 vm((2, groups, 4, part, wide), bf16),
-                vm((groups, 4, part, width), bf16),
+                vm((8, 16, hidden), bf16),
                 vm((4, 16, hidden), bf16),
                 vm((2, 8, groups, part, hidden), bf16),
-                vm((8, groups, part, width), bf16),
+                vm((8, 16, hidden), bf16),
                 vm((8, 16, hidden // 2), bf16),
                 vm((2, groups, groups, part, hidden), bf16),
-                vm((groups, groups, part, width), bf16),
+                vm((groups, 16, hidden), bf16),
                 vm((groups, 16, hidden // 2), bf16),
                 vm((2, groups, 4, part, wide), f32),
-                vm((groups, 4, part, width), f32),
+                vm((8, 16, hidden), f32),
                 vm((4, 16, hidden), f32),
                 vm((2, hidden, wide), f32),
-                vm((hidden, width), f32),
-                sem((2 * graphs,)),
+                vm((128, hidden), f32),
+                sem((graphs + 2,)),
                 sem((6, 10)),
                 sem((6, 10)),
                 sem((ROUNDS, 7)),
                 sem((ROUNDS, 7)),
                 sem((13, groups - 1)),
                 sem((13, groups - 1)),
+                sem((2, groups - 1)),
+                sem((2, groups - 1)),
                 sem((4, 7)),
                 sem((4, 7)),
                 sem((4, 7)),
@@ -1036,17 +1092,17 @@
             ),
             name="train_step",
         )(
-            features,
+            jnp.transpose(features, (2, 0, 1)),
             adjacency,
             labels,
             train_mask,
-            input_weight,
-            input_moment,
-            conv_weight,
-            conv_moment,
-            head_weight,
-            head_first,
-            head_second,
+            input_weight.T,
+            input_moment.T,
+            jnp.swapaxes(conv_weight, 1, 2),
+            jnp.swapaxes(conv_moment, 1, 2),
+            head_weight.T,
+            head_first.T,
+            head_second.T,
             head_bias[None, :],
             bias_first[None, :],
             bias_second[None, :],
@@ -1054,25 +1110,35 @@
             norm_first,
             norm_second,
         )
-        small, in_new, in_m, conv_new, conv_m, h_new, h_f, h_s, n_new, n_f, n_s = outs
+        outs = pl.pallas_call(
+            hand_over,
+            out_shape=results,
+            in_specs=[near] * 14,
+            out_specs=[near] * 14,
+            name="hand_over",
+        )(*outs)
+        loss, in_new, in_m, conv_new, conv_m, h_new, h_f, h_s, b_new, b_f, b_s, *norms = outs
         return (
-            small[3, :2],
-            in_new,
-            in_m,
-            conv_new,
-            conv_m,
-            h_new,
-            h_f,
-            h_s,
-            small[0, :classes],
-            small[1, :classes],
-            small[2, :classes],
-            n_new,
-            n_f,
-            n_s,
+            loss[0],
+            in_new.T,
+            in_m.T,
+            jnp.swapaxes(conv_new, 1, 2),
+            jnp.swapaxes(conv_m, 1, 2),
+            h_new.T,
+            h_f.T,
+            h_s.T,
+            b_new[0],
+            b_f[0],
+            b_s[0],
+            *norms,
         )
 
     return call
+
+
+def hand_over(*refs):
+    for source, target in zip(refs[:14], refs[14:]):
+        target[...] = source[...]
 
 
 def solution(mesh):

time: 148 us -> 113 us (0.76)
  local copies, waits for them, and re-layouts: 31.3 us -> 0 us
  Pallas kernels: 116 us -> 112 us
    unnamed x18 -> x0, local copies, waits for them, and re-layouts: 28.8 us -> none
    pallas_call x1, Pallas kernels: 116 us -> 110 us  [call(): pl.pallas_call(functools.partial(step_kernel, groups, classes), out_shape...]
    squeeze x2 -> x0, local copies, waits for them, and re-layouts: 2.49 us -> none  [the longest x1 1.31 us: call(): small[2, :classes]]
    pallas_call x0 -> x1, Pallas kernels: none -> 2.04 us  [call(): pl.pallas_call(hand_over, out_shape=results, in_specs=[near] * 14, out_sp...]
where the time goes in v2:
time: 113 us
  Pallas kernels  112 us (99%)
    pallas_call x1, Pallas kernels, call(): pl.pallas_call(functools.partial(step_kernel, groups, classes), out_shape...  110 us

profile of v2, /device:TPU:0, one launch (start us, length us, event | category | flops | bytes accessed | tf_op | source)
XLA Modules:
  0.0 113.2 jit_solution(9989779145235993828)
XLA Ops:
  0.7 110.5 %train_step.1 = (f32[1,2]{1,0:T(1,128)}, f32[64,100]{1,0:T(8,128)}, f32[64,100]{1,0:T(8,128)}, f32[2,64,512]{2,1,0:T(8,128)}, f32[2,64,512]{2,1,0:T(8,128)}, /*i...) custom-call(bf16[100,2,512]{2,1,0:T(2,128)(2,1)} %bitcast.24, ...), custom_call_target="tpu_custom_call" | custom-call | tf_op jit(solution)/shard_map/train_step/pallas_call | solution.py:1024
  111.1 2.0 %hand_over.1 = (f32[1,2]{1,0:T(1,128)}, f32[64,100]{1,0:T(8,128)}, f32[64,100]{1,0:T(8,128)}, f32[2,64,512]{2,1,0:T(8,128)}, f32[2,64,512]{2,1,0:T(8,128)}, /*in...) custom-call(f32[1,2]{1,0:T(1,128)} %get-tuple-element.42.refs_0_, ...), custom_call_target="tpu_custom_call" | custom-call | tf_op jit(solution)/shard_map/hand_over/pallas_call | solution.py:1113

commit v3 on v2

--- a/solution.py
+++ b/solution.py
@@ -243,6 +243,7 @@
 NN = (((1,), (0,)), ((), ()))
 VMEM_BYTES = 56 * 1024 * 1024
 ROUNDS = 8
+EARLY_STEPS = 0
 
 
 def flip(index, bit):
@@ -440,12 +441,18 @@
 
         kept = {}
 
-        def own():
+        def own_first():
             kept[0] = go(0, n_x, me, low)
             kept[1] = go(1, n_y, me, high)
             kept[6] = go(6, n_sib, me)
+
+        def own_second():
             kept[2] = go(2, n_x, me, high)
             kept[3] = go(3, n_y, me, low)
+
+        def own():
+            own_first()
+            own_second()
 
         def relay():
             kept[0].wait_recv()
@@ -471,7 +478,7 @@
         def far_ready():
             kept[9].wait_recv()
 
-        return own, relay, near, far, near_ready, far_ready
+        return own, relay, near, far, near_ready, far_ready, own_first, own_second
 
     def chip_at(i):
         cx = lax.rem(lax.rem(chip, 2) + lax.rem(i, 2), 2)
@@ -774,9 +781,10 @@
     x_g[1][3]()
     x_g[1][5]()
     product_x(1, 3, 4)
+    count_plane = normalise(0, 0, 0, hg.at[0, me])
+    h_g[0][6]()
     layer_zero(1)
-    count_plane = normalise(0, 0, 0, hg.at[0, me])
-    h_g[0][0]()
+    h_g[0][7]()
     zs[0, g] = count_plane
     z_send(3, zs.at[0, g])
     z_forward(1, wb)
@@ -792,62 +800,62 @@
     h_g[0][4]()
     product(0, hg.at[0], acc, 0, 3)
     h_g[0][3]()
-    h_g[1][1]()
     h_g[0][5]()
     product(0, hg.at[0], acc, 3, 4)
     layer_one(0)
+    h_g[1][1]()
     z_wait(3)
     count = zs[0, 0]
     for i in range(1, groups):
         count = count + zs[0, i]
     count = count[2:3, 0:1]
+    h_g[1][2]()
     normalise(0, 1, 2, h2.at[0])
     loss_row = head(0, count)
     backward_sums(0, 1, 4, loss_row)
-    h_g[1][2]()
     h_g[1][3]()
-    backward_pre(0, 1, 4)
-    dg[0, me] = lowered(dot(dp[1, 0], wb[:, hidden:]))
-    d_g[0][0]()
     h_g[1][4]()
     product(1, hg.at[1], acc, 0, 3)
     h_g[1][5]()
     product(1, hg.at[1], acc, 3, 4)
     layer_one(1)
-    conv_grads(0, 1, hg[0, me], agg[1, 0])
+    backward_pre(0, 1, 4)
+    dg[0, me] = lowered(dot(dp[1, 0], wb[:, hidden:]))
+    d_g[0][0]()
     dh[0] = dot(dp[1, 0], wb[:, :hidden])
     normalise(1, 1, 3, h2.at[1])
     loss_row = head(1, count)
     backward_sums(1, 1, 5, loss_row)
     d_g[0][1]()
+    conv_grads(0, 1, hg[0, me], agg[1, 0])
     backward_pre(1, 1, 5)
     dg[1, me] = lowered(dot(dp[1, 1], wb[:, hidden:]))
     d_g[1][0]()
-    conv_grads(1, 1, hg[1, me], agg[1, 1])
+    d_g[0][2]()
     dh[1] = dot(dp[1, 1], wb[:, :hidden])
-    gbc[1] = lowered(gt[1]).reshape(groups, 4, part, wide)
-    gbh[...] = lowered(ght[...]).reshape(4, 16, hidden)
     zs[1, g] = sums[0]
     z_send(4, zs.at[1, g])
-    d_g[0][2]()
     d_g[0][4]()
     product(0, dg.at[0], acc, 0, 3)
     d_g[0][3]()
-    d_g[1][1]()
     d_g[0][5]()
     product(0, dg.at[0], acc, 3, 4)
     dh[0] = lowered(dh[0] + acc[...]).astype(f32)
     backward_sums(0, 0, 6)
+    d_g[1][1]()
+    conv_grads(1, 1, hg[1, me], agg[1, 1])
+    gbc[1] = lowered(gt[1]).reshape(groups, 4, part, wide)
+    gbh[...] = lowered(ght[...]).reshape(4, 16, hidden)
     pieces_send(0, gbc.at[1], rsc.at[1], conv_piece)
     pieces_send(1, gbh, rsh, head_piece)
     d_g[1][2]()
-    d_g[1][4]()
-    product(1, dg.at[1], acc, 0, 3)
-    d_g[1][3]()
     backward_pre(0, 0, 6)
     turned = conv_grads(0, 0, h0[0], agg[0, 0])
     q1[...] = dot(turned, xg[0, me], NT)
     q2[...] = dot(turned, axh[0])
+    d_g[1][4]()
+    product(1, dg.at[1], acc, 0, 3)
+    d_g[1][3]()
     d_g[1][5]()
     product(1, dg.at[1], acc, 3, 4)
     dh[1] = lowered(dh[1] + acc[...]).astype(f32)
@@ -856,12 +864,18 @@
     z_send(9, zc.at[1, g])
     zh[g] = lowered(pieces_sum(1, None, rsh, head_piece(gbh, me)[...]))
     z_send(10, zh.at[g])
+    z_wait(6)
+    z_wait(7)
+    z_wait(8)
+    tall_in[...] = mit[...]
+    mi[...] = tall_in[...].T.reshape(8, 16, hidden)
+    tall_in[...] = jnp.zeros_like(tall_in)
     backward_pre(1, 0, 7)
     turned = conv_grads(1, 0, h0[1], agg[0, 1])
+    gbc[0] = lowered(gt[0]).reshape(groups, 4, part, wide)
+    pieces_send(2, gbc.at[0], rsc.at[0], conv_piece)
     q1[...] += dot(turned, xg[1, me], NT)
     q2[...] += dot(turned, axh[1])
-    gbc[0] = lowered(gt[0]).reshape(groups, 4, part, wide)
-    pieces_send(2, gbc.at[0], rsc.at[0], conv_piece)
     one, two = split(q1[...]), split(q2[...])
     w_self, w_near = wn[0, :hidden, :], wn[0, hidden:, :]
     g_in = dot(w_self, one[0]) + dot(w_self, one[1]) + dot(w_near, two[0]) + dot(w_near, two[1])
@@ -880,65 +894,56 @@
     def in_view(node):
         return mfi.at[node]
 
-    z_wait(7)
+    def scaled(value):
+        norm = jnp.sqrt(jnp.sum(jnp.sum(value * value, 0, keepdims=True), 1, keepdims=True))
+        return value / (norm + 1e-07)
+
+    def iterate(refs, first, last):
+        for i in range(first, last):
+            for ref in refs:
+                value = ref[...]
+                pair = split(value)
+                gram = dot_three(pair, pair, NT)
+                gram_high, gram_rest = split(gram)
+                cross = dot(gram_high, gram_rest)
+                square = dot(gram_high, gram_high) + cross + cross.T
+                poly = split(poly_second * gram + poly_third * square)
+                ref[...] = poly_first * value + dot_three(poly, pair)
+
+    factor_conv = 0.2 * float(wide) ** 0.5
+    factor_in = 0.2 * float(max(width, hidden)) ** 0.5
+
+    def conv_out(l):
+        o_conv_m[l] = mf[l, g].reshape(shard, wide)
+        ortho = y_conv[l, own_rows, :]
+        weight = w_conv[l]
+        o_conv[l] = weight - muon_rate * (factor_conv * ortho + decay_rate * weight)
+
     mf[1, :, chip, :, core_lanes] = muon_beta * mpc[1] + over_z(9, zc.at[1])
     spread(0, conv_view(1))
     hf[chip, :, head_lanes] = over_z(10, zh)
     spread(1, head_view)
-    z_wait(6)
-    z_wait(8)
-    tall_in[...] = mit[...]
-    mi[...] = tall_in[...].T.reshape(8, 16, hidden)
     zc[0, g] = lowered(pieces_sum(2, None, rsc.at[0], conv_piece(gbc.at[0], me)[...]))
     z_send(11, zc.at[0, g])
     zi[g] = lowered(pieces_sum(3, None, rsi, gbi[me]))
     z_send(12, zi.at[g])
     spread_forward(0, conv_view(1))
     spread_forward(1, head_view)
+    spread_wait(0)
+    y_conv[1] = scaled(mf[1].reshape(hidden, wide))
+    iterate([y_conv.at[1]], 0, EARLY_STEPS)
     mf[0, :, chip, :, core_lanes] = muon_beta * mpc[0] + over_z(11, zc.at[0])
     spread(2, conv_view(0))
     mfi[me] = muon_beta * mi[me] + over_z(12, zi)
     spread(3, in_view)
-
-    def scaled(value):
-        norm = jnp.sqrt(jnp.sum(jnp.sum(value * value, 0, keepdims=True), 1, keepdims=True))
-        return value / (norm + 1e-07)
-
-    def iterate(refs):
-        def body(i, carry):
-            for ref in refs:
-                value = ref[...]
-                pair = split(value)
-                gram = dot_three(pair, pair, NT)
-                gram_pair = split(gram)
-                poly = split(poly_second * gram + poly_third * dot_three(gram_pair, gram_pair))
-                ref[...] = poly_first * value + dot_three(poly, pair)
-            return carry
-
-        lax.fori_loop(0, NS_STEPS, body, 0)
-
-    factor_conv = 0.2 * float(wide) ** 0.5
-    factor_in = 0.2 * float(max(width, hidden)) ** 0.5
-
-    def conv_out(l):
-        o_conv_m[l] = mf[l, g].reshape(shard, wide)
-        ortho = y_conv[l, own_rows, :]
-        weight = w_conv[l]
-        o_conv[l] = weight - muon_rate * (factor_conv * ortho + decay_rate * weight)
-
-    spread_wait(0)
-    y_conv[1] = scaled(mf[1].reshape(hidden, wide))
-    iterate([y_conv.at[1]])
+    iterate([y_conv.at[1]], EARLY_STEPS, NS_STEPS)
     spread_forward(2, conv_view(0))
     spread_forward(3, in_view)
     conv_out(1)
 
-    def adam(weight, grad, first, second):
-        return adamw(weight, grad, first, second)
-
     spread_wait(1)
     grad = hf[...].reshape(64, hidden)[:classes]
-    o_head[...], o_head_f[...], o_head_s[...] = adam(w_head[...], grad, f_head[...], s_head[...])
+    o_head[...], o_head_f[...], o_head_s[...] = adamw(w_head[...], grad, f_head[...], s_head[...])
     z_wait(4)
     z_wait(5)
     late = zs[1, 0]
@@ -948,8 +953,8 @@
         early = early + zs[2, i]
     for l, rows_l in ((0, early), (1, late)):
         grad = jnp.concatenate([rows_l[1:2], rows_l[0:1]], 0)
-        o_norm[l], o_norm_f[l], o_norm_s[l] = adam(w_norm[l], grad, f_norm[l], s_norm[l])
-    o_bias[...], o_bias_f[...], o_bias_s[...] = adam(
+        o_norm[l], o_norm_f[l], o_norm_s[l] = adamw(w_norm[l], grad, f_norm[l], s_norm[l])
+    o_bias[...], o_bias_f[...], o_bias_s[...] = adamw(
         w_bias[...], late[2:3, :classes], f_bias[...], s_bias[...]
     )
     o_loss[...] = jnp.concatenate([late[3:4, 0:1], count], 1)
@@ -958,7 +963,7 @@
     spread_wait(3)
     y_conv[0] = scaled(mf[0].reshape(hidden, wide))
     y_in[...] = scaled(mfi[...].reshape(128, hidden))
-    iterate([y_conv.at[0], y_in])
+    iterate([y_conv.at[0], y_in], 0, NS_STEPS)
     conv_out(0)
     tall_in[...] = mfi[...].reshape(128, hidden).T
     o_in_m[...] = tall_in[own_rows, :][:, :width]

time: 113 us -> 104 us (0.920)
  Pallas kernels: 112 us -> 103 us
    pallas_call x1, Pallas kernels: 110 us -> 101 us  [call(): pl.pallas_call(functools.partial(step_kernel, groups, classes), out_shape...]
where the time goes in v3:
time: 104 us
  Pallas kernels  103 us (99%)
    pallas_call x1, Pallas kernels, call(): pl.pallas_call(functools.partial(step_kernel, groups, classes), out_shape...  101 us

profile of v3, /device:TPU:0, one launch (start us, length us, event | category | flops | bytes accessed | tf_op | source)
XLA Modules:
  0.0 104.1 jit_solution(6974363615657400382)
XLA Ops:
  0.7 101.3 %train_step.1 = (f32[1,2]{1,0:T(1,128)}, f32[64,100]{1,0:T(8,128)}, f32[64,100]{1,0:T(8,128)}, f32[2,64,512]{2,1,0:T(8,128)}, f32[2,64,512]{2,1,0:T(8,128)}, /*i...) custom-call(bf16[100,2,512]{2,1,0:T(2,128)(2,1)} %bitcast.24, ...), custom_call_target="tpu_custom_call" | custom-call | tf_op jit(solution)/shard_map/train_step/pallas_call | solution.py:1029
  101.9 2.0 %hand_over.1 = (f32[1,2]{1,0:T(1,128)}, f32[64,100]{1,0:T(8,128)}, f32[64,100]{1,0:T(8,128)}, f32[2,64,512]{2,1,0:T(8,128)}, f32[2,64,512]{2,1,0:T(8,128)}, /*in...) custom-call(f32[1,2]{1,0:T(1,128)} %get-tuple-element.42.refs_0_, ...), custom_call_target="tpu_custom_call" | custom-call | tf_op jit(solution)/shard_map/hand_over/pallas_call | solution.py:1118

commit v4 on v3

--- a/solution.py
+++ b/solution.py
@@ -384,20 +384,20 @@
     peers = [n_d, flip(n_d, 1), n_x, n_y, flip(n_x, 1), flip(n_y, 1), n_sib]
     z_peers = [lax.rem(g + d, groups) for d in range(1, groups)]
     z_from = [lax.rem(g + groups - d, groups) for d in range(1, groups)]
-    started = []
+    sent = []
 
     def send(src, dst, s_sem, r_sem, group, node):
-        copy = pltpu.make_async_remote_copy(
+        pltpu.make_async_remote_copy(
             src_ref=src,
             dst_ref=dst,
             send_sem=s_sem,
             recv_sem=r_sem,
             device_id=(group, node),
             device_id_type=MESH,
-        )
-        copy.start()
-        started.append(copy)
-        return copy
+        ).start()
+
+    def drain(sem, view):
+        pltpu.make_async_copy(view, view, sem).wait()
 
     def lanes_of_core(span):
         return pl.ds(pl.multiple_of(core * span, span), span)
@@ -433,50 +433,49 @@
     def gather_of(index, ref, by_lane=False):
         low, high = pl.ds(0, half), pl.ds(half, half)
 
-        def go(j, node, block, span=None):
+        def go(r, node, block, span=None):
             view = ref.at[block]
             if span is not None:
                 view = ref.at[block, :, span] if by_lane else ref.at[block, span]
-            return send(view, view, ga_s.at[index, j], ga_r.at[index, j], g, node)
-
-        kept = {}
+            send(view, view, ga_s.at[index], ga_r.at[5 * index + r], g, node)
+
+        def arrived(r, blocks):
+            drain(ga_r.at[5 * index + r], ref.at[pl.ds(0, blocks)])
+
+        sent.append((ga_s.at[index], ref.at[pl.ds(0, 7)]))
 
         def own_first():
-            kept[0] = go(0, n_x, me, low)
-            kept[1] = go(1, n_y, me, high)
-            kept[6] = go(6, n_sib, me)
+            go(0, n_x, me, low)
+            go(0, n_y, me, high)
+            go(3, n_sib, me)
 
         def own_second():
-            kept[2] = go(2, n_x, me, high)
-            kept[3] = go(3, n_y, me, low)
+            go(1, n_x, me, high)
+            go(1, n_y, me, low)
 
         def own():
             own_first()
             own_second()
 
         def relay():
-            kept[0].wait_recv()
-            kept[4] = go(4, n_y, n_x, low)
-            kept[1].wait_recv()
-            kept[5] = go(5, n_x, n_y, high)
+            arrived(0, 1)
+            go(2, n_y, n_x, low)
+            go(2, n_x, n_y, high)
 
         def near():
-            kept[2].wait_recv()
-            kept[7] = go(7, n_sib, n_x)
-            kept[3].wait_recv()
-            kept[8] = go(8, n_sib, n_y)
+            arrived(1, 1)
+            go(3, n_sib, n_x)
+            go(3, n_sib, n_y)
 
         def far():
-            kept[4].wait_recv()
-            kept[5].wait_recv()
-            kept[9] = go(9, n_sib, n_d)
+            arrived(2, 1)
+            go(4, n_sib, n_d)
 
         def near_ready():
-            for j in (6, 7, 8):
-                kept[j].wait_recv()
+            arrived(3, 3)
 
         def far_ready():
-            kept[9].wait_recv()
+            arrived(4, 1)
 
         return own, relay, near, far, near_ready, far_ready, own_first, own_second
 
@@ -519,33 +518,31 @@
     def fold(value):
         return jnp.sum(value.reshape(chunk // 8, 8, hidden), 0)
 
-    st_copies = {}
-
     def plane_send(k):
         view = st.at[k, me]
-        st_copies[k] = [
-            send(view, view, st_s.at[k, i], st_r.at[k, i], g, node) for i, node in enumerate(peers)
-        ]
+        for node in peers:
+            send(view, view, st_s.at[k], st_r.at[k], g, node)
+        sent.append((st_s.at[k], st.at[k, pl.ds(0, 7)]))
 
     def plane_sum(k):
-        for copy in st_copies[k]:
-            copy.wait_recv()
+        drain(st_r.at[k], st.at[k, pl.ds(0, 7)])
         value = st[k, 0]
         for i in range(1, 8):
             value = value + st[k, i]
         return value
 
-    z_copies = {}
-
-    def z_send(k, view):
-        z_copies[k] = [
-            send(view, view, z_s.at[k, i], z_r.at[k, i], group, me)
-            for i, group in enumerate(z_peers)
-        ]
+    z_all = {}
+
+    def z_send(k, view, all_views):
+        for group in z_peers:
+            send(view, view, z_s.at[k], z_r.at[k], group, me)
+        z_all[k] = all_views
+        sent.append((z_s.at[k], all_views))
 
     def z_wait(k):
-        for copy in z_copies[k]:
-            copy.wait_recv()
+        drain(z_r.at[k], z_all[k])
+
+    others = pl.ds(0, groups - 1)
 
     x_g = [gather_of(s, xg.at[s], True) for s in range(2)]
     h_g = [gather_of(2 + s, hg.at[s]) for s in range(2)]
@@ -557,25 +554,24 @@
     def strip_of(group):
         return pl.ds(pl.multiple_of(group * shard + core * strip, strip), strip)
 
-    forwards = {}
+    strips = pl.ds(0, strip * (groups - 1))
 
     def z_forward(k, ref):
-        forwards[k] = []
-        for i, group in enumerate(z_from):
-            z_copies[k][i].wait_recv()
+        z_wait(k)
+        for group in z_from:
             view = ref.at[strip_of(group)]
-            forwards[k].append(send(view, view, zf_s.at[k, i], zf_r.at[k, i], g, n_sib))
+            send(view, view, zf_s.at[k], zf_r.at[k], g, n_sib)
+        sent.append((zf_s.at[k], ref.at[strips]))
 
     def z_forwarded(k):
-        for copy in forwards[k]:
-            copy.wait_recv()
+        drain(zf_r.at[k], z_all[k])
 
     x_g[0][0]()
-    z_send(0, wa.at[strip_of(g)])
+    z_send(0, wa.at[strip_of(g)], wa.at[strips])
     mit[high_rows, pl.ds(0, width)] = m_in[...]
     x_g[0][1]()
     x_g[1][0]()
-    z_send(1, wb.at[strip_of(g)])
+    z_send(1, wb.at[strip_of(g)], wb.at[strips])
     padh[...] = jnp.zeros_like(padh)
     padh[pl.ds(0, classes), pl.ds(0, hidden)] = w_head[...]
     wt_head[...] = lowered(padh[:, :hidden])
@@ -706,19 +702,14 @@
             gt[l, :, hidden:] += two
         return turned
 
-    rs_copies = {}
-
     def pieces_send(k, src, dst, where):
-        rs_copies[k] = []
-        for i, node in enumerate(peers):
-            rs_copies[k].append(
-                send(where(src, node), dst.at[me], rs_s.at[k, i], rs_r.at[k, i], g, node)
-            )
+        for node in peers:
+            send(where(src, node), dst.at[me], rs_s.at[k], rs_r.at[k], g, node)
+        sent.append((rs_s.at[k], dst.at[pl.ds(0, 7)]))
 
     def pieces_sum(k, src, dst, own):
         dst[me] = own
-        for copy in rs_copies[k]:
-            copy.wait_recv()
+        drain(rs_r.at[k], dst.at[pl.ds(0, 7)])
         value = dst[0].astype(f32)
         for i in range(1, 8):
             value = value + dst[i].astype(f32)
@@ -742,36 +733,32 @@
             value = value + buf[i].astype(f32)
         return value
 
-    ag_copies = {}
-
-    def spread(k, view_of):
+    def spread(k, view_of, some):
         view = view_of(me)
-        ag_copies[k] = [
-            send(view, view, ag_s.at[k, i], ag_r.at[k, i], g, node)
-            for i, node in enumerate((n_d, n_x, n_y, n_sib))
-        ]
-
-    def spread_forward(k, view_of):
-        for i, node in ((1, n_x), (2, n_y), (0, n_d)):
-            ag_copies[k][i].wait_recv()
+        for node in (n_d, n_x, n_y):
+            send(view, view, ag_s.at[k], ag_r.at[2 * k], g, node)
+        send(view, view, ag_s.at[k], ag_r.at[2 * k + 1], g, n_sib)
+        sent.append((ag_s.at[k], some(4)))
+
+    def spread_forward(k, view_of, some):
+        drain(ag_r.at[2 * k], some(3))
+        for node in (n_x, n_y, n_d):
             view = view_of(node)
-            ag_copies[k].append(
-                send(view, view, ag_s.at[k, 4 + i], ag_r.at[k, 4 + i], g, n_sib)
-            )
-
-    def spread_wait(k):
-        for copy in ag_copies[k][3:]:
-            copy.wait_recv()
+            send(view, view, ag_s.at[4 + k], ag_r.at[2 * k + 1], g, n_sib)
+        sent.append((ag_s.at[4 + k], some(3)))
+
+    def spread_wait(k, some):
+        drain(ag_r.at[2 * k + 1], some(4))
 
     head_lanes = lanes_of_core(hidden // 2)
 
     x_g[0][4]()
     product_x(0, 0, 3)
-    x_g[1][1]()
     x_g[0][3]()
     z_forward(0, wa)
     x_g[0][5]()
     product_x(0, 3, 4)
+    x_g[1][1]()
     z_forwarded(0)
     wn[0] = wa[:, :wide].T
     layer_zero(0)
@@ -786,14 +773,14 @@
     layer_zero(1)
     h_g[0][7]()
     zs[0, g] = count_plane
-    z_send(3, zs.at[0, g])
+    z_send(3, zs.at[0, g], zs.at[0, others])
     z_forward(1, wb)
     normalise(1, 0, 1, hg.at[1, me])
     h_g[0][1]()
     h_g[1][0]()
-    z_send(6, mpc.at[0, g])
-    z_send(7, mpc.at[1, g])
-    z_send(8, mit.at[own_rows])
+    z_send(6, mpc.at[0, g], mpc.at[0, others])
+    z_send(7, mpc.at[1, g], mpc.at[1, others])
+    z_send(8, mit.at[own_rows], mit.at[pl.ds(0, shard * (groups - 1))])
     z_forwarded(1)
     wn[1] = wb[...].T
     h_g[0][2]()
@@ -834,7 +821,7 @@
     d_g[0][2]()
     dh[1] = dot(dp[1, 1], wb[:, :hidden])
     zs[1, g] = sums[0]
-    z_send(4, zs.at[1, g])
+    z_send(4, zs.at[1, g], zs.at[1, others])
     d_g[0][4]()
     product(0, dg.at[0], acc, 0, 3)
     d_g[0][3]()
@@ -861,9 +848,9 @@
     dh[1] = lowered(dh[1] + acc[...]).astype(f32)
     backward_sums(1, 0, 7)
     zc[1, g] = lowered(pieces_sum(0, None, rsc.at[1], conv_piece(gbc.at[1], me)[...]))
-    z_send(9, zc.at[1, g])
+    z_send(9, zc.at[1, g], zc.at[1, others])
     zh[g] = lowered(pieces_sum(1, None, rsh, head_piece(gbh, me)[...]))
-    z_send(10, zh.at[g])
+    z_send(10, zh.at[g], zh.at[others])
     z_wait(6)
     z_wait(7)
     z_wait(8)
@@ -883,10 +870,19 @@
     gbi[...] = lowered(tall_in[...].T).reshape(8, 16, hidden)
     pieces_send(3, gbi, rsi, in_piece)
     zs[2, g] = sums[1]
-    z_send(5, zs.at[2, g])
+    z_send(5, zs.at[2, g], zs.at[2, others])
 
     def conv_view(l):
         return lambda node: conv_piece(mf.at[l], node)
+
+    def conv_some(l):
+        return lambda n: mf.at[l, :, pl.ds(0, n), :, pl.ds(0, hidden)]
+
+    def head_some(n):
+        return hf.at[pl.ds(0, n), :, pl.ds(0, hidden // 2)]
+
+    def in_some(n):
+        return mfi.at[pl.ds(0, n)]
 
     def head_view(node):
         return head_piece(hf, node)
@@ -920,28 +916,28 @@
         o_conv[l] = weight - muon_rate * (factor_conv * ortho + decay_rate * weight)
 
     mf[1, :, chip, :, core_lanes] = muon_beta * mpc[1] + over_z(9, zc.at[1])
-    spread(0, conv_view(1))
+    spread(0, conv_view(1), conv_some(1))
     hf[chip, :, head_lanes] = over_z(10, zh)
-    spread(1, head_view)
+    spread(1, head_view, head_some)
     zc[0, g] = lowered(pieces_sum(2, None, rsc.at[0], conv_piece(gbc.at[0], me)[...]))
-    z_send(11, zc.at[0, g])
+    z_send(11, zc.at[0, g], zc.at[0, others])
     zi[g] = lowered(pieces_sum(3, None, rsi, gbi[me]))
-    z_send(12, zi.at[g])
-    spread_forward(0, conv_view(1))
-    spread_forward(1, head_view)
-    spread_wait(0)
+    z_send(12, zi.at[g], zi.at[others])
+    spread_forward(0, conv_view(1), conv_some(1))
+    spread_forward(1, head_view, head_some)
+    spread_wait(0, conv_some(1))
     y_conv[1] = scaled(mf[1].reshape(hidden, wide))
     iterate([y_conv.at[1]], 0, EARLY_STEPS)
     mf[0, :, chip, :, core_lanes] = muon_beta * mpc[0] + over_z(11, zc.at[0])
-    spread(2, conv_view(0))
+    spread(2, conv_view(0), conv_some(0))
     mfi[me] = muon_beta * mi[me] + over_z(12, zi)
-    spread(3, in_view)
+    spread(3, in_view, in_some)
     iterate([y_conv.at[1]], EARLY_STEPS, NS_STEPS)
-    spread_forward(2, conv_view(0))
-    spread_forward(3, in_view)
+    spread_forward(2, conv_view(0), conv_some(0))
+    spread_forward(3, in_view, in_some)
     conv_out(1)
 
-    spread_wait(1)
+    spread_wait(1, head_some)
     grad = hf[...].reshape(64, hidden)[:classes]
     o_head[...], o_head_f[...], o_head_s[...] = adamw(w_head[...], grad, f_head[...], s_head[...])
     z_wait(4)
@@ -959,8 +955,8 @@
     )
     o_loss[...] = jnp.concatenate([late[3:4, 0:1], count], 1)
 
-    spread_wait(2)
-    spread_wait(3)
+    spread_wait(2, conv_some(0))
+    spread_wait(3, in_some)
     y_conv[0] = scaled(mf[0].reshape(hidden, wide))
     y_in[...] = scaled(mfi[...].reshape(128, hidden))
     iterate([y_conv.at[0], y_in], 0, NS_STEPS)
@@ -971,8 +967,8 @@
     ortho = tall_in[own_rows, :][:, :width]
     weight = w_in[...]
     o_in[...] = weight - muon_rate * (factor_in * ortho + decay_rate * weight)
-    for copy in started:
-        copy.wait_send()
+    for sem, view in sent:
+        drain(sem, view)
 
 
 def planned(mesh):
@@ -1079,18 +1075,18 @@
                 vm((2, hidden, wide), f32),
                 vm((128, hidden), f32),
                 sem((graphs + 2,)),
-                sem((6, 10)),
-                sem((6, 10)),
-                sem((ROUNDS, 7)),
-                sem((ROUNDS, 7)),
-                sem((13, groups - 1)),
-                sem((13, groups - 1)),
-                sem((2, groups - 1)),
-                sem((2, groups - 1)),
-                sem((4, 7)),
-                sem((4, 7)),
-                sem((4, 7)),
-                sem((4, 7)),
+                sem((6,)),
+                sem((30,)),
+                sem((ROUNDS,)),
+                sem((ROUNDS,)),
+                sem((13,)),
+                sem((13,)),
+                sem((2,)),
+                sem((2,)),
+                sem((4,)),
+                sem((4,)),
+                sem((8,)),
+                sem((8,)),
             ],
             compiler_params=pltpu.CompilerParams(
                 collective_id=0, has_side_effects=True, vmem_limit_bytes=VMEM_BYTES

time: 104 us -> 101 us (0.971)
  Pallas kernels: 103 us -> 99.9 us
    pallas_call x1, Pallas kernels: 101 us -> 97.9 us  [call(): pl.pallas_call(functools.partial(step_kernel, groups, classes), out_shape...]
where the time goes in v4:
time: 101 us
  Pallas kernels  99.9 us (99%)
    pallas_call x1, Pallas kernels, call(): pl.pallas_call(functools.partial(step_kernel, groups, classes), out_shape...  97.9 us
    pallas_call x1, Pallas kernels, call(): pl.pallas_call(hand_over, out_shape=results, in_specs=[near] * 14, out_sp...  2.04 us

profile of v4, /device:TPU:0, one launch (start us, length us, event | category | flops | bytes accessed | tf_op | source)
XLA Modules:
  0.0 100.7 jit_solution(1685469446883588228)
XLA Ops:
  0.7 97.9 %train_step.1 = (f32[1,2]{1,0:T(1,128)}, f32[64,100]{1,0:T(8,128)}, f32[64,100]{1,0:T(8,128)}, f32[2,64,512]{2,1,0:T(8,128)}, f32[2,64,512]{2,1,0:T(8,128)}, /*i...) custom-call(bf16[100,2,512]{2,1,0:T(2,128)(2,1)} %bitcast.24, ...), custom_call_target="tpu_custom_call" | custom-call | tf_op jit(solution)/shard_map/train_step/pallas_call | solution.py:1025
  98.5 2.0 %hand_over.1 = (f32[1,2]{1,0:T(1,128)}, f32[64,100]{1,0:T(8,128)}, f32[64,100]{1,0:T(8,128)}, f32[2,64,512]{2,1,0:T(8,128)}, f32[2,64,512]{2,1,0:T(8,128)}, /*in...) custom-call(f32[1,2]{1,0:T(1,128)} %get-tuple-element.42.refs_0_, ...), custom_call_target="tpu_custom_call" | custom-call | tf_op jit(solution)/shard_map/hand_over/pallas_call | solution.py:1114

commit v5 on v4

--- a/solution.py
+++ b/solution.py
@@ -502,12 +502,13 @@
             accx[...] = jnp.zeros_like(accx)
 
         def body(i, carry):
-            block = 2 * chip_at(lax.div(i, 2)) + lax.rem(i, 2)
-            left = av[s, :, pl.ds(pl.multiple_of(block * rows, rows), rows)]
-            accx[...] += dot(left, xg[s, block], NT)
+            c = chip_at(i)
+            left = av[s, :, pl.ds(pl.multiple_of(c * 2 * rows, 2 * rows), 2 * rows)]
+            right = jnp.concatenate([xg[s, 2 * c], xg[s, 2 * c + 1]], 1)
+            accx[...] += dot(left, right, NT)
             return carry
 
-        lax.fori_loop(2 * first, 2 * last, body, 0)
+        lax.fori_loop(first, last, body, 0)
 
     def over_rows(body, carry):
         def one(i, value):
@@ -518,7 +519,11 @@
     def fold(value):
         return jnp.sum(value.reshape(chunk // 8, 8, hidden), 0)
 
-    def plane_send(k):
+    def plane_send(k, lines):
+        side = hidden // 2
+        for i, line in enumerate(lines):
+            st[k, me, 2 * i : 2 * i + 1, :] = line[:, :side]
+            st[k, me, 2 * i + 1 : 2 * i + 2, :] = line[:, side:]
         view = st.at[k, me]
         for node in peers:
             send(view, view, st_s.at[k], st_r.at[k], g, node)
@@ -529,7 +534,8 @@
         value = st[k, 0]
         for i in range(1, 8):
             value = value + st[k, i]
-        return value
+        lines = [jnp.concatenate([value[i : i + 1], value[i + 1 : i + 2]], 1) for i in (0, 2, 4, 6)]
+        return jnp.concatenate([*lines, jnp.zeros((4, hidden), f32)], 0)
 
     z_all = {}
 
@@ -587,7 +593,7 @@
         copy.wait()
 
     def forward_act(s, l, k, first, second, w_first, w_second):
-        acc[...] = dot(first, w_first) + dot(second, w_second)
+        acc[...] = dot(first, w_first, NT) + dot(second, w_second, NT)
 
         def body(span, carry):
             pre = acc[span, :]
@@ -603,12 +609,10 @@
 
         zero = jnp.zeros((8, hidden), f32)
         one, two = over_rows(body, (zero, zero))
-        st[k, me] = jnp.zeros((8, hidden), f32)
-        st[k, me, 0:1, :] = jnp.sum(one, 0, keepdims=True)
-        st[k, me, 1:2, :] = jnp.sum(two, 0, keepdims=True)
-        if k == 0:
-            st[k, me, 2:3, :] = jnp.broadcast_to(count_own, (1, hidden))
-        plane_send(k)
+        lines = [jnp.sum(one, 0, keepdims=True), jnp.sum(two, 0, keepdims=True)]
+        none = jnp.zeros((1, hidden), f32)
+        lines.append(jnp.broadcast_to(count_own, (1, hidden)) if k == 0 else none)
+        plane_send(k, lines + [none])
 
     def normalise(s, l, k, out):
         sums_all = plane_sum(k)
@@ -633,11 +637,11 @@
         w = wa[:, wide : wide + span_in]
         agg[0, s] = lowered(dot(high, w, NT) + dot(rest, w, NT))
         h0[s] = lowered(dot(xg[s, me].T, w, NT))
-        forward_act(s, 0, s, h0[s], agg[0, s], wn[0, :hidden, :], wn[0, hidden:, :])
+        forward_act(s, 0, s, h0[s], agg[0, s], wa[:, :hidden], wa[:, hidden:wide])
 
     def layer_one(s):
         agg[1, s] = lowered(acc[...])
-        forward_act(s, 1, 2 + s, hg[s, me], agg[1, s], wn[1, :hidden, :], wn[1, hidden:, :])
+        forward_act(s, 1, 2 + s, hg[s, me], agg[1, s], wb[:, :hidden], wb[:, hidden:])
 
     def head(s, count):
         value = h2[s]
@@ -668,13 +672,14 @@
 
         zero = jnp.zeros((8, hidden), f32)
         one, two = over_rows(body, (zero, zero))
-        st[k, me] = jnp.zeros((8, hidden), f32)
-        st[k, me, 0:1, :] = jnp.sum(one, 0, keepdims=True)
-        st[k, me, 1:2, :] = jnp.sum(two, 0, keepdims=True)
-        if extra is not None:
-            st[k, me, 2:3, 0:64] = extra[1][0:1]
-            st[k, me, 3:4, :] = jnp.broadcast_to(extra[0], (1, hidden))
-        plane_send(k)
+        lines = [jnp.sum(one, 0, keepdims=True), jnp.sum(two, 0, keepdims=True)]
+        if extra is None:
+            lines += [jnp.zeros((1, hidden), f32)] * 2
+        else:
+            rest = jnp.zeros((1, hidden - 64), f32)
+            lines.append(jnp.concatenate([extra[1][0:1], rest], 1))
+            lines.append(jnp.broadcast_to(extra[0], (1, hidden)))
+        plane_send(k, lines)
 
     def backward_pre(s, l, k):
         sums_all = plane_sum(k)
@@ -760,7 +765,6 @@
     product_x(0, 3, 4)
     x_g[1][1]()
     z_forwarded(0)
-    wn[0] = wa[:, :wide].T
     layer_zero(0)
     x_g[1][2]()
     x_g[1][4]()
@@ -782,7 +786,7 @@
     z_send(7, mpc.at[1, g], mpc.at[1, others])
     z_send(8, mit.at[own_rows], mit.at[pl.ds(0, shard * (groups - 1))])
     z_forwarded(1)
-    wn[1] = wb[...].T
+    wn[...] = wa[:, :wide].T
     h_g[0][2]()
     h_g[0][4]()
     product(0, hg.at[0], acc, 0, 3)
@@ -864,7 +868,7 @@
     q1[...] += dot(turned, xg[1, me], NT)
     q2[...] += dot(turned, axh[1])
     one, two = split(q1[...]), split(q2[...])
-    w_self, w_near = wn[0, :hidden, :], wn[0, hidden:, :]
+    w_self, w_near = wn[:hidden, :], wn[hidden:, :]
     g_in = dot(w_self, one[0]) + dot(w_self, one[1]) + dot(w_near, two[0]) + dot(w_near, two[1])
     tall_in[:, pl.ds(0, span_in)] = g_in
     gbi[...] = lowered(tall_in[...].T).reshape(8, 16, hidden)
@@ -1036,7 +1040,7 @@
                 vm((128, rows), f32),
                 vm((hidden, wide + 128), bf16),
                 vm((hidden, wide), bf16),
-                vm((2, wide, hidden), bf16),
+                vm((wide, hidden), bf16),
                 vm((128, hidden), bf16),
                 vm((graphs, rows, hidden), bf16),
                 vm((2, graphs, rows, hidden), bf16),
@@ -1054,7 +1058,7 @@
                 vm((hidden, span_in), f32),
                 vm((hidden, 128), f32),
                 vm((64, hidden), f32),
-                vm((ROUNDS, 8, 8, hidden), f32),
+                vm((ROUNDS, 8, 8, hidden // 2), f32),
                 vm((3, groups, 8, hidden), f32),
                 vm((2, 8, hidden), f32),
                 vm((2, groups, part, hidden), f32),

time: 101 us -> 98.3 us (0.973)
  Pallas kernels: 99.9 us -> 97.3 us
    pallas_call x1, Pallas kernels: 97.9 us -> 95.2 us  [call(): pl.pallas_call(functools.partial(step_kernel, groups, classes), out_shape...]
where the time goes in v5:
time: 98.3 us; the launch traced here: 98.1 us
  Pallas kernels  97.3 us (99%)
    pallas_call x1, Pallas kernels, call(): pl.pallas_call(functools.partial(step_kernel, groups, classes), out_shape...  95.2 us
    pallas_call x1, Pallas kernels, call(): pl.pallas_call(hand_over, out_shape=results, in_specs=[near] * 14, out_sp...  2.04 us

profile of v5, /device:TPU:0, one launch (start us, length us, event | category | flops | bytes accessed | tf_op | source)
XLA Modules:
  0.0 98.1 jit_solution(4945808108219167309)
XLA Ops:
  0.7 95.2 %train_step.1 = (f32[1,2]{1,0:T(1,128)}, f32[64,100]{1,0:T(8,128)}, f32[64,100]{1,0:T(8,128)}, f32[2,64,512]{2,1,0:T(8,128)}, f32[2,64,512]{2,1,0:T(8,128)}, /*i...) custom-call(bf16[100,2,512]{2,1,0:T(2,128)(2,1)} %bitcast.24, ...), custom_call_target="tpu_custom_call" | custom-call | tf_op jit(solution)/shard_map/train_step/pallas_call | solution.py:1029
  95.9 2.0 %hand_over.1 = (f32[1,2]{1,0:T(1,128)}, f32[64,100]{1,0:T(8,128)}, f32[64,100]{1,0:T(8,128)}, f32[2,64,512]{2,1,0:T(8,128)}, f32[2,64,512]{2,1,0:T(8,128)}, /*in...) custom-call(f32[1,2]{1,0:T(1,128)} %get-tuple-element.42.refs_0_, ...), custom_call_target="tpu_custom_call" | custom-call | tf_op jit(solution)/shard_map/hand_over/pallas_call | solution.py:1118

commit v6 on v5

--- a/solution.py
+++ b/solution.py
@@ -273,23 +273,23 @@
 def step_kernel(
     groups,
     classes,
-    feat,
+    feat_far,
     adj,
-    labels,
-    train,
-    w_in,
-    m_in,
-    w_conv,
+    labels_far,
+    train_far,
+    w_in_far,
+    m_in_far,
+    w_conv_far,
     m_conv,
-    w_head,
-    f_head,
-    s_head,
-    w_bias,
-    f_bias,
-    s_bias,
-    w_norm,
-    f_norm,
-    s_norm,
+    w_head_far,
+    f_head_far,
+    s_head_far,
+    w_bias_far,
+    f_bias_far,
+    s_bias_far,
+    w_norm_far,
+    f_norm_far,
+    s_norm_far,
     o_loss,
     o_in,
     o_in_m,
@@ -350,6 +350,21 @@
     hf,
     y_conv,
     y_in,
+    feat,
+    w_in,
+    w_conv,
+    labels,
+    train,
+    m_in,
+    w_head,
+    f_head,
+    s_head,
+    w_bias,
+    f_bias,
+    s_bias,
+    w_norm,
+    f_norm,
+    s_norm,
     loc,
     ga_s,
     ga_r,
@@ -408,6 +423,29 @@
     for group in z_peers:
         pl.semaphore_signal(barrier, inc=1, device_id=(group, me), device_id_type=MESH)
 
+    far_refs = (
+        (feat_far, feat),
+        (w_in_far, w_in),
+        (w_conv_far, w_conv),
+        (labels_far, labels),
+        (train_far, train),
+        (m_in_far, m_in),
+        (w_head_far, w_head),
+        (f_head_far, f_head),
+        (s_head_far, s_head),
+        (w_bias_far, w_bias),
+        (f_bias_far, f_bias),
+        (s_bias_far, s_bias),
+        (w_norm_far, w_norm),
+        (f_norm_far, f_norm),
+        (s_norm_far, s_norm),
+    )
+    own_in = [
+        pltpu.make_async_copy(far, here, loc.at[graphs + 2 + i])
+        for i, (far, here) in enumerate(far_refs)
+    ]
+    for copy in own_in:
+        copy.start()
     own_a = [pltpu.make_async_copy(adj.at[s], av.at[s], loc.at[s]) for s in range(graphs)]
     part_rows = pl.ds(pl.multiple_of(chip * part, part), part)
     core_lanes = lanes_of_core(hidden)
@@ -420,10 +458,12 @@
 
     high_rows = pl.ds(pl.multiple_of(g * shard, shard), shard)
     padh[...] = jnp.zeros_like(padh)
+    mit[...] = jnp.zeros_like(mit)
+    for copy in own_in[:3]:
+        copy.wait()
     for s in range(graphs):
         padh[pl.ds(0, width), :] = feat[:, s, :].astype(f32)
         xg[s, me] = lowered(padh[pl.ds(0, span_in), :])
-    mit[...] = jnp.zeros_like(mit)
     mit[high_rows, pl.ds(0, width)] = w_in[...]
     wa[high_rows, pl.ds(0, wide)] = lowered(w_conv[0])
     wa[high_rows, pl.ds(wide, 128)] = lowered(mit[high_rows, :])
@@ -574,6 +614,8 @@
 
     x_g[0][0]()
     z_send(0, wa.at[strip_of(g)], wa.at[strips])
+    for copy in own_in[3:]:
+        copy.wait()
     mit[high_rows, pl.ds(0, width)] = m_in[...]
     x_g[0][1]()
     x_g[1][0]()
@@ -1029,7 +1071,7 @@
         outs = pl.pallas_call(
             functools.partial(step_kernel, groups, classes),
             out_shape=results,
-            in_specs=[near, anywhere, near, near, near, near, near, anywhere] + [near] * 9,
+            in_specs=[anywhere] * 17,
             out_specs=[near] * 14,
             scratch_shapes=[
                 vm((graphs, rows, total), bf16),
@@ -1078,7 +1120,22 @@
                 vm((4, 16, hidden), f32),
                 vm((2, hidden, wide), f32),
                 vm((128, hidden), f32),
-                sem((graphs + 2,)),
+                vm((width, graphs, rows), bf16),
+                vm((shard, width), f32),
+                vm((2, shard, wide), f32),
+                vm((graphs, rows), jnp.int32),
+                vm((graphs, rows), jnp.int32),
+                vm((shard, width), f32),
+                vm((classes, hidden), f32),
+                vm((classes, hidden), f32),
+                vm((classes, hidden), f32),
+                vm((1, classes), f32),
+                vm((1, classes), f32),
+                vm((1, classes), f32),
+                vm(norm_params.shape, f32),
+                vm(norm_params.shape, f32),
+                vm(norm_params.shape, f32),
+                sem((graphs + 17,)),
                 sem((6,)),
                 sem((30,)),
                 sem((ROUNDS,)),

time: 98.3 us -> 97.3 us (0.990)
  Pallas kernels: 97.3 us -> 96.3 us
where the time goes in v6:
time: 97.3 us; the launch traced here: 97.1 us
  Pallas kernels  96.3 us (99%)
    pallas_call x1, Pallas kernels, call(): pl.pallas_call(functools.partial(step_kernel, groups, classes), out_shape...  94.3 us
    pallas_call x1, Pallas kernels, call(): pl.pallas_call(hand_over, out_shape=results, in_specs=[near] * 14, out_sp...  2.04 us

profile of v6, /device:TPU:0, one launch (start us, length us, event | category | flops | bytes accessed | tf_op | source)
XLA Modules:
  0.0 97.1 jit_solution(13755034657448631579)
XLA Ops:
  0.7 94.3 %train_step.1 = (f32[1,2]{1,0:T(1,128)}, f32[64,100]{1,0:T(8,128)}, f32[64,100]{1,0:T(8,128)}, f32[2,64,512]{2,1,0:T(8,128)}, f32[2,64,512]{2,1,0:T(8,128)}, /*i...) custom-call(bf16[100,2,512]{2,1,0:T(2,128)(2,1)} %bitcast.24, ...), custom_call_target="tpu_custom_call" | custom-call | tf_op jit(solution)/shard_map/train_step/pallas_call | solution.py:1071
  94.9 2.0 %hand_over.1 = (f32[1,2]{1,0:T(1,128)}, f32[64,100]{1,0:T(8,128)}, f32[64,100]{1,0:T(8,128)}, f32[2,64,512]{2,1,0:T(8,128)}, f32[2,64,512]{2,1,0:T(8,128)}, /*in...) custom-call(f32[1,2]{1,0:T(1,128)} %get-tuple-element.42.refs_0_, ...), custom_call_target="tpu_custom_call" | custom-call | tf_op jit(solution)/shard_map/hand_over/pallas_call | solution.py:1175

commit v7 on v6

--- a/solution.py
+++ b/solution.py
@@ -389,7 +389,7 @@
     part = shard // 4
     half = rows // 2
     span_in = 16 * ((width + 15) // 16)
-    chunk = min(rows, 128)
+    chunk = min(rows, 512)
     chunks = rows // chunk
     g = lax.axis_index("grp")
     me = lax.axis_index("node")

time: 97.3 us -> 96.6 us (level)
  no operation moved by 1% of the time
where the time goes in v7:
time: 96.6 us; the launch traced here: 96.4 us
  Pallas kernels  95.6 us (99%)
    pallas_call x1, Pallas kernels, call(): pl.pallas_call(functools.partial(step_kernel, groups, classes), out_shape...  93.6 us
    pallas_call x1, Pallas kernels, call(): pl.pallas_call(hand_over, out_shape=results, in_specs=[near] * 14, out_sp...  2.04 us

profile of v7, /device:TPU:0, one launch (start us, length us, event | category | flops | bytes accessed | tf_op | source)
XLA Modules:
  0.0 96.4 jit_solution(4693628771154893887)
XLA Ops:
  0.7 93.6 %train_step.1 = (f32[1,2]{1,0:T(1,128)}, f32[64,100]{1,0:T(8,128)}, f32[64,100]{1,0:T(8,128)}, f32[2,64,512]{2,1,0:T(8,128)}, f32[2,64,512]{2,1,0:T(8,128)}, /*i...) custom-call(bf16[100,2,512]{2,1,0:T(2,128)(2,1)} %bitcast.24, ...), custom_call_target="tpu_custom_call" | custom-call | tf_op jit(solution)/shard_map/train_step/pallas_call | solution.py:1071
  94.2 2.0 %hand_over.1 = (f32[1,2]{1,0:T(1,128)}, f32[64,100]{1,0:T(8,128)}, f32[64,100]{1,0:T(8,128)}, f32[2,64,512]{2,1,0:T(8,128)}, f32[2,64,512]{2,1,0:T(8,128)}, /*in...) custom-call(f32[1,2]{1,0:T(1,128)} %get-tuple-element.42.refs_0_, ...), custom_call_target="tpu_custom_call" | custom-call | tf_op jit(solution)/shard_map/hand_over/pallas_call | solution.py:1175
